TPU v7x, 256 devices: a whole 4x4x8 slice. The times are simulated.
256 devices in a mesh: blk: 16 (over x_hi, z), group: 16 (over x_lo, y, core).
Axes of the slice: x: 4 (x_hi: 2, x_lo: 2; x = x_hi * 2 + x_lo), y: 4, z: 8, core: 2. Of those that a mesh axis runs over, the one named last changes fastest.
Arguments:
- q_embed: bfloat16 [16, 2048, 1024], P('group', 'blk'), may hold values from -24 to 24
- t_embed: bfloat16 [16, 2048, 1024], P('group', 'blk'), may hold values from -24 to 24
- head: bfloat16 [1024, 1024], replicated, may hold values from -0.1875 to 0.1875
- positive: int32 [16, 2048], P('group', 'blk'), may hold values from 0 to 2047, each once within a row
- hard_ids: int32 [16, 2048, 4], P('group', 'blk'), may hold values from 0 to 32767, as said below
- loss_weight: float32 [16, 2048], P('group', 'blk'), may hold values from 1 to 8
Outputs:
- grad_q: bfloat16 [16, 2048, 1024], P('group', 'blk')
- grad_t: bfloat16 [16, 2048, 1024], P('group', 'blk')
- grad_head: float32 [1024, 1024], P(('blk', 'group'))
Inputs may be any that keep to these rules, and one draw needn't show every extreme that they name: hard_ids[g, i, k] = g2 * 2048 + j names a table of another group g2 != g whose row j lies in the same block of 128 rows as i. Of the 512 slots (i, k) of one block of 128 rows, at most 70 name tables of any one group, and exactly 70 slots name tables of some group in every block; several slots may name the same table.
All inputs are finite; a program needn't handle non-finite values.
Results may differ from a plain program's by a relative error of at most 0.014.
Values may be sent and summed in bfloat16 or wider, within the bound.
A program may use at most 64 MiB of HBM per device.

v0:
```python
import jax
import jax.numpy as jnp
from jax import lax
from jax.sharding import PartitionSpec as P


def dot_rows(left, right):
    return lax.dot_general(
        left, right, (((1,), (1,)), ((), ())), preferred_element_type=jnp.float32
    )


def dot_cols(left, right):
    return lax.dot_general(
        left, right, (((0,), (0,)), ((), ())), preferred_element_type=jnp.float32
    )


def body(q_embed, t_embed, head, positive, hard_ids, loss_weight):
    inputs = q_embed[0]
    tables_in = t_embed[0]
    row_count = inputs.shape[0]
    feat_width = inputs.shape[1]
    logit_scale = feat_width ** (-0.5)
    blocks = lax.axis_size("blk")
    groups = lax.axis_size("group")
    cycle_index = lax.axis_index("blk")
    pair_count = row_count * blocks
    hard_count = hard_ids.shape[2]
    capacity = 2 * ((hard_count * row_count + groups - 2) // (groups - 1))
    queries = jnp.dot(inputs, head, preferred_element_type=jnp.float32).astype(jnp.bfloat16)
    table_keys = jnp.dot(tables_in, head, preferred_element_type=jnp.float32).astype(jnp.bfloat16)
    group_keys = lax.all_gather(table_keys, "blk", axis=0, tiled=True)
    wanted = hard_ids[0].reshape(-1)
    owner_group = wanted // pair_count
    local_row = wanted % pair_count - cycle_index * row_count
    owner_hot = (owner_group[:, None] == jnp.arange(groups, dtype=jnp.int32)[None, :]).astype(
        jnp.int32
    )
    before = jnp.cumsum(owner_hot, axis=0) - owner_hot
    slot_rank = jnp.sum(before * owner_hot, axis=1)
    placing = owner_group * capacity + slot_rank
    requests = (
        jnp.zeros((groups * capacity,), jnp.int32)
        .at[placing]
        .set(local_row)
        .reshape(groups, capacity)
    )
    incoming = lax.all_to_all(requests, "group", split_axis=0, concat_axis=0, tiled=True)
    found_rows = table_keys[incoming]
    returned = lax.all_to_all(found_rows, "group", split_axis=0, concat_axis=0, tiled=True)
    negatives = returned.reshape(groups * capacity, feat_width)[placing].reshape(
        row_count, hard_count, feat_width
    )
    scores = logit_scale * dot_rows(queries, group_keys)
    hard_scores = logit_scale * jnp.einsum(
        "re,rke->rk", queries, negatives, preferred_element_type=jnp.float32
    )
    row_max = jnp.maximum(jnp.max(scores, axis=1), jnp.max(hard_scores, axis=1))
    row_total = jnp.sum(jnp.exp(scores - row_max[:, None]), axis=1) + jnp.sum(
        jnp.exp(hard_scores - row_max[:, None]), axis=1
    )
    log_total = row_max + jnp.log(row_total)
    weight_row = loss_weight[0]
    target_row = positive[0]
    is_target = (target_row[:, None] == jnp.arange(pair_count, dtype=jnp.int32)[None, :]).astype(
        jnp.float32
    )
    score_grad = (weight_row[:, None] * (jnp.exp(scores - log_total[:, None]) - is_target)).astype(
        jnp.bfloat16
    )
    hard_grad = (weight_row[:, None] * jnp.exp(hard_scores - log_total[:, None])).astype(
        jnp.bfloat16
    )
    query_grad = logit_scale * (
        jnp.dot(score_grad, group_keys, preferred_element_type=jnp.float32)
        + jnp.einsum("rk,rke->re", hard_grad, negatives, preferred_element_type=jnp.float32)
    )
    query_grad = query_grad.astype(jnp.bfloat16)
    hard_rows = (
        logit_scale
        * hard_grad.astype(jnp.float32)[:, :, None]
        * queries.astype(jnp.float32)[:, None, :]
    ).astype(jnp.bfloat16)
    outgoing = (
        jnp.zeros((groups * capacity, feat_width), jnp.bfloat16)
        .at[placing]
        .set(hard_rows.reshape(-1, feat_width))
    )
    received = lax.all_to_all(
        outgoing.reshape(groups, capacity, feat_width),
        "group",
        split_axis=0,
        concat_axis=0,
        tiled=True,
    )
    slot_rows = incoming.reshape(-1)
    pick_table = (jnp.arange(row_count, dtype=jnp.int32)[:, None] == slot_rows[None, :]).astype(
        jnp.bfloat16
    )
    table_hard = jnp.dot(
        pick_table, received.reshape(-1, feat_width), preferred_element_type=jnp.float32
    )
    table_in = lax.psum_scatter(
        (logit_scale * dot_cols(score_grad, queries)).astype(jnp.bfloat16),
        "blk",
        scatter_dimension=0,
        tiled=True,
    ).astype(jnp.float32)
    table_grad = (table_in + table_hard).astype(jnp.bfloat16)
    grad_q = dot_rows(query_grad, head).astype(jnp.bfloat16)
    grad_t = dot_rows(table_grad, head).astype(jnp.bfloat16)
    grad_head = lax.psum_scatter(
        dot_cols(inputs, query_grad) + dot_cols(tables_in, table_grad),
        ("blk", "group"),
        scatter_dimension=0,
        tiled=True,
    )
    return (grad_q[None], grad_t[None], grad_head)


def solution(mesh):
    in_specs = (
        P("group", "blk", None),
        P("group", "blk", None),
        P(),
        P("group", "blk"),
        P("group", "blk", None),
        P("group", "blk"),
    )
    out_specs = (P("group", "blk", None), P("group", "blk", None), P(("blk", "group"), None))
    return jax.shard_map(body, mesh=mesh, in_specs=in_specs, out_specs=out_specs, check_vma=False)
```

profile of v0, /device:TPU:1, one launch (start us, length us, event | category | flops | bytes accessed | tf_op | source)
XLA Modules:
  0.0 616.8 jit_solution(13759940827621835648)
XLA Ops:
  7.2 0.0 copy-start
  7.2 0.0 copy-start.6
  7.2 0.0 all-gather.2.cloned.1.call-start
  7.2 1.5 copy-done
  8.8 2.1 convolution_convert_fusion.2
  10.9 0.0 all-gather.2.cloned.1.call-update
  10.9 0.1 copy.15
  11.0 0.1 reshape_squeeze.8
  11.1 0.1 reshape_squeeze.9
  11.2 0.1 reshape_squeeze.7
  11.4 1.2 reduce-window.6
  12.5 0.2 slice_reduce_fusion
  12.8 0.1 fusion.20
  12.9 2.5 scatter_custom_fusion
  15.4 0.1 all_to_all.14
  15.5 12.2 %all_to_all.22 = s32[16,1,70]{2,1,0:T(1,128)S(1)} all-to-all(s32[16,1,70]{2,1,0:T(1,128)S(1)} %all_to_all.14), channel_id=1, replica_groups=mesh['blk'=16,'group'=16] {'group'}, dimensions={0} | all-to-all | bytes 8960 | tf_op jit(solution)/shard_map/all_to_all | solution.py:49
  27.7 0.1 reshape.202
  27.8 0.0 copy-done.1
  27.8 5.0 gather_fusion
  32.7 4.1 reshape.201
  36.9 5.0 all-to-all-start.1
  41.9 0.2 reduce-scatter.3.cloned.1.call-start
  42.1 0.0 copy-done.2
  42.1 0.4 convolution_convert_fusion.3
  42.6 33.2 %all-to-all-done.1 = bf16[16,70,1024]{2,1,0:T(8,128)(2,1)} async-done(((bf16[16,70,1024]{2,1,0:T(8,128)(2,1)}), bf16[16,70,1024]{2,1,0:T(8,128)(2,1)}, u32[]{:S(2)}, u32[]{:S(2)}) %all-to-all-start.1) | async-done | bytes 2293792 | tf_op jit(solution)/shard_map/all_to_all | solution.py:51
  75.8 4.2 reshape.196
  79.9 4.7 gather_fusion.1
  84.6 1.2 reshape.197
  85.8 2.4 fusion.8
  88.2 0.1 multiply_reduce_fusion
  88.3 0.0 copy-start.5
  88.3 0.0 copy-start.7
  88.3 29.5 %all-gather.2.cloned.1.call-done = bf16[2048,1024]{1,0:T(8,128)(2,1)} async-done(((bf16[128,1024]{1,0:T(8,128)(2,1)}), bf16[2048,1024]{1,0:T(8,128)(2,1)}) %all-gather.2.cloned.1.call-update) | async-done | bytes 4194320 | tf_op jit(solution)/shard_map/all_gather | solution.py:33
  117.8 3.8 fusion.29
  121.6 0.2 exponential_reduce_fusion.1
  121.8 0.3 exponential_reduce_fusion
  122.1 3.4 multiply_convert_fusion
  125.5 0.0 reduce-scatter.3.cloned.1.call-update
  125.5 1.9 mul.104
  127.5 3.0 mul.105
  130.4 0.1 convert_multiply_fusion
  130.6 0.1 mul.102
  130.7 5.4 scatter_custom_fusion.1
  136.1 4.1 reshape.198
  140.2 9.3 %all-to-all-start.2 = ((bf16[16,70,1024]{2,1,0:T(8,128)(2,1)}), bf16[16,70,1024]{2,1,0:T(8,128)(2,1)}, u32[]{:S(2)}, u32[]{:S(2)}) async-start(bf16[16,70,1024]{2,1,0:T(8,128)(2,1)} %reshape.198), calls=%async_computation.3 | async-start | bytes 4718592 | tf_op jit(solution)/shard_map/all_to_all | solution.py:90
  149.5 0.3 all-reduce.3.cloned.1.call-start
  149.7 0.5 broadcast.175
  150.3 0.7 reduce.5
  150.9 0.1 eq.64
  151.0 1.9 fusion.16
  152.9 0.0 copy-start.3
  153.0 3.2 fusion.1
  156.2 2.7 fusion.13
  158.9 23.9 %all-to-all-done.2 = bf16[16,70,1024]{2,1,0:T(8,128)(2,1)} async-done(((bf16[16,70,1024]{2,1,0:T(8,128)(2,1)}), bf16[16,70,1024]{2,1,0:T(8,128)(2,1)}, u32[]{:S(2)}, u32[]{:S(2)}) %all-to-all-start.2) | async-done | bytes 2293792 | tf_op jit(solution)/shard_map/all_to_all | solution.py:90
  182.8 4.1 reshape.199
  186.9 144.7 %reduce-scatter.3.cloned.1.call-done = bf16[128,1024]{1,0:T(8,128)(2,1)} async-done(((bf16[2048,1024]{1,0:T(8,128)(2,1)}), bf16[128,1024]{1,0:T(8,128)(2,1)}) %reduce-scatter.3.cloned.1.call-update) | async-done | bytes 262160 | tf_op jit(solution)/shard_map/reduce_scatter | solution.py:104
  331.6 2.2 fusion.2
  333.8 4.8 add_bitcast_fusion
  338.6 0.0 all-reduce.3.cloned.1.call-update
  338.7 1.5 fusion.3
  340.2 1.5 fusion.4
  341.7 266.6 %all-reduce.3.cloned.1.call-done = f32[1024,1024]{0,1:T(8,128)} async-done(((f32[1024,1024]{0,1:T(8,128)}), f32[1024,1024]{0,1:T(8,128)}) %all-reduce.3.cloned.1.call-update) | async-done | bytes 4194320
  608.3 1.2 constant_dynamic-slice_fusion
  609.5 0.8 copy.19
  (19 shorter events, 0.1 us)
Async XLA Ops:
  7.2 1.6 copy-start
  7.2 3.7 copy-start.6
  7.2 110.6 %all-gather.2.cloned.1.call-start = ((), (), s32[]{:S(2)}) async-start(), calls=%async_computation.4 | async-start | bytes 4456448 | tf_op jit(solution)/shard_map/all_gather | solution.py:33
  10.9 16.9 %copy-start.1 = (bf16[128,1024]{1,0:T(8,128)(2,1)S(1)}, bf16[128,1024]{1,0:T(8,128)(2,1)}, u32[]{:S(2)}) copy-start(bf16[128,1024]{1,0:T(8,128)(2,1)} %convolution_convert_fusion.2) | copy-start | bytes 786436
  36.9 5.2 copy-start.2
  36.9 38.9 %all-to-all-start.1 = ((bf16[16,70,1024]{2,1,0:T(8,128)(2,1)}), bf16[16,70,1024]{2,1,0:T(8,128)(2,1)}, u32[]{:S(2)}, u32[]{:S(2)}) async-start(bf16[16,70,1024]{2,1,0:T(8,128)(2,1)} %reshape.201), calls=%async_computation.1 | async-start | bytes 4718592 | tf_op jit(solution)/shard_map/all_to_all | solution.py:51
  41.9 289.7 %reduce-scatter.3.cloned.1.call-start = ((), (), s32[]{:S(2)}) async-start(), calls=%async_computation.5 | async-start | bytes 4456448 | tf_op jit(solution)/shard_map/reduce_scatter | solution.py:104
  88.3 33.8 %copy-start.5 = (f32[1,128]{1,0:T(1,128)S(1)}, f32[1,128]{1,0:T(1,128)}, u32[]{:S(2)}) copy-start(f32[1,128]{1,0:T(1,128)} %param.11) | copy-start | bytes 1540
  88.3 33.8 %copy-start.7 = (s32[1,128]{1,0:T(1,128)S(1)}, s32[1,128]{1,0:T(1,128)}, u32[]{:S(2)}) copy-start(s32[1,128]{1,0:T(1,128)} %param.9) | copy-start | bytes 1540
  140.2 42.6 %all-to-all-start.2 = ((bf16[16,70,1024]{2,1,0:T(8,128)(2,1)}), bf16[16,70,1024]{2,1,0:T(8,128)(2,1)}, u32[]{:S(2)}, u32[]{:S(2)}) async-start(bf16[16,70,1024]{2,1,0:T(8,128)(2,1)} %reshape.198), calls=%async_computation.3 | async-start | bytes 4718592 | tf_op jit(solution)/shard_map/all_to_all | solution.py:90
  149.5 458.8 %all-reduce.3.cloned.1.call-start = ((), (), s32[]{:S(2)}) async-start(), calls=%async_computation.6 | async-start | bytes 8388608
  152.9 3.2 copy-start.3
  186.9 146.8 %copy-start.4 = (bf16[1,128,1024]{2,1,0:T(8,128)(2,1)S(1)}, bf16[1,128,1024]{2,1,0:T(8,128)(2,1)}, u32[]{:S(2)}) copy-start(bf16[1,128,1024]{2,1,0:T(8,128)(2,1)} %param.7) | copy-start | bytes 786436
Sparse Core Ops, SparseCore 0:
  11.2 106.5 all-gather.1
  125.7 205.8 reduce-scatter.2
  338.8 269.4 all-reduce.2
where the time goes:
time: 619 us; the launch traced here: 617 us
  waiting for transfers between devices  498 us (80%)
  local copies, waits for them, and re-layouts  39.9 us (6%)
  matrix products  30 us (5%)
  starting transfers between devices  14.8 us (2%)
  between operations  14 us (2%)
  blocking collectives  12.2 us (2%)
  other arithmetic  8.13 us (1%)
    unnamed x4, waiting for transfers between devices  267 us
    reduce_scatter x1, waiting for transfers between devices, body(): lax.psum_scatter((logit_scale * dot_cols(score_grad, queries)).astype(jnp...  145 us
    all_to_all x1, waiting for transfers between devices, body(): lax.all_to_all(found_rows, 'group', split_axis=0, concat_axis=0, tiled=True)  33.2 us
    all_gather x1, waiting for transfers between devices, body(): group_keys = lax.all_gather(table_keys, 'blk', axis=0, tiled=True)  29.5 us
    all_to_all x1, waiting for transfers between devices, body(): lax.all_to_all(outgoing.reshape(groups, capacity, feat_width), 'group', s...  23.9 us
  transfers between devices with their start and end apart: 5, of which 5 were waited for; matrix products, arithmetic and copies ran while one was open for 9% of the time, Pallas kernels for 0%

commit v1 on v0

v1 whole, which is shorter than its diff:
```python
import functools
import math

import jax
import jax.numpy as jnp
from jax import lax
from jax.experimental import pallas as pl
from jax.experimental.pallas import tpu as pltpu
from jax.sharding import PartitionSpec as P

MESH = pl.DeviceIdType.MESH
F32 = jnp.float32
BF16 = jnp.bfloat16

NZ = 8
NY = 4
NEG = -1e30


Z_AG, Y_AG, C_AG, X_IN, STAT = 0, 8, 12, 16, 20
Z_RS, C_RS, Y_RS, X_OUT = 23, 31, 35, 39
H_C, H_Y, H_X, H_Z, H_C2 = 41, 42, 45, 48, 55
COPIES = 56


def nn(left, right):
    return lax.dot_general(left, right, (((1,), (0,)), ((), ())), preferred_element_type=F32)


def nt(left, right):
    return lax.dot_general(left, right, (((1,), (1,)), ((), ())), preferred_element_type=F32)


def tn(left, right):
    return lax.dot_general(left, right, (((0,), (0,)), ((), ())), preferred_element_type=F32)


def span(i, size):
    return pl.ds(pl.multiple_of(i * size, size), size)


def loop(count, unroll=1):
    def run(step):
        lax.fori_loop(0, count, lambda i, carry: (step(i), carry)[1], 0, unroll=unroll)
    return run


def kernel(
    qe_ref, te_ref, head_ref, meta_ref, gq_ref, gt_ref, gh_ref,
    xa, qq, qp, tz, ty, meta, s_in, s_hd, g_in, g_hd, st_in, st_hd, stat, lse,
    zs, zr, zown, cs, cr, yown, ys, yr, acc, qgs, qgr,
    h2, hcs, hcr, hys, hyr, hxs, hxr, hzs, hzr, hc2s, hc2r,
    send_sem, recv_sem,
):
    rows, feat = qe_ref.shape
    half = rows // 2
    scale = feat ** -0.5
    cols = NZ * rows
    fhalf = feat // 2
    blk, grp = lax.axis_index("blk"), lax.axis_index("group")
    xh, z = lax.div(blk, NZ), lax.rem(blk, NZ)
    xl, y, c = lax.div(grp, 2 * NY), lax.rem(lax.div(grp, 2), NY), lax.rem(grp, 2)

    def at(dz=0, dy=0, dx=0, dc=0):
        xh2 = 1 - xh if dx & 2 else xh
        xl2 = 1 - xl if dx & 1 else xl
        c2 = 1 - c if dc else c
        z2, y2 = lax.rem(z + dz + NZ, NZ), lax.rem(y + dy + NY, NY)
        return (xh2 * NZ + z2, (xl2 * NY + y2) * 2 + c2)

    def copy(src, dst, sem, device):
        return pltpu.make_async_remote_copy(
            src_ref=src, dst_ref=dst, send_sem=send_sem.at[sem], recv_sem=recv_sem.at[sem],
            device_id=device, device_id_type=MESH,
        )

    peers = (
        [at(dz=d) for d in range(1, NZ)] + [at(dy=d) for d in range(1, NY)]
        + [at(dx=d) for d in (1, 2, 3)] + [at(dc=1)]
    )
    barrier = pltpu.get_barrier_semaphore()
    for peer in peers:
        pl.semaphore_signal(barrier, inc=1, device_id=peer, device_id_type=MESH)
    pl.semaphore_wait(barrier, len(peers))

    started = []

    def start(*args):
        one = copy(*args)
        one.start()
        started.append(one)
        return one

    zright, zleft = at(dz=1), at(dz=-1)
    yright, yleft = at(dy=1), at(dy=-1)
    core = at(dc=1)
    lo, hi = pl.ds(0, half), pl.ds(half, half)

    zag_r, zag_l = {}, {}
    zag_r[1] = start(te_ref, tz.at[NZ - 1], Z_AG + 0, zright)
    zag_l[1] = start(te_ref, tz.at[1], Z_AG + 1, zleft)
    x1 = start(qe_ref, xa.at[pl.ds(0, rows)], X_IN + 0, at(dx=1))
    x2 = start(qe_ref, xa.at[pl.ds(2 * rows, rows)], X_IN + 1, at(dx=2))
    yag_r = start(te_ref, ty.at[3], Y_AG + 0, yright)
    yag_l = start(te_ref, ty.at[1], Y_AG + 1, yleft)
    cag = [start(te_ref, ty.at[4], C_AG + 0, core)]
    m1 = start(meta_ref, meta.at[pl.ds(0, rows)], X_IN + 2, at(dx=1))
    m2 = start(meta_ref, meta.at[pl.ds(2 * rows, rows)], X_IN + 3, at(dx=2))

    tz[0] = te_ref[...]
    ty[0] = te_ref[...]
    xa[pl.ds(rows, rows), :] = qe_ref[...]
    meta[pl.ds(rows, rows), :] = meta_ref[...]

    def project(first, count):
        own = pl.ds(first, count)

        def forward(i):
            part = nn(xa[own, :], head_ref[:, span(i, 256)]).astype(BF16)
            qq[lax.div(i, 2), pl.ds(3 * rows + first, count), span(lax.rem(i, 2), 256)] = part

        loop(feat // 256)(forward)

        def back(i):
            block = span(i, 256)
            total = nt(qq[0, pl.ds(3 * rows + first, count), :], head_ref[block, pl.ds(0, fhalf)])
            total += nt(qq[1, pl.ds(3 * rows + first, count), :], head_ref[block, pl.ds(fhalf, fhalf)])
            qp[own, block] = (scale * total).astype(BF16)

        loop(feat // 256)(back)

    def z_pass(step):
        zag_r[step].wait_recv()
        zag_l[step].wait_recv()
        if step < 3:
            zag_r[step + 1] = start(tz.at[NZ - step], tz.at[NZ - step - 1], Z_AG + 2 * step, zright)
            zag_l[step + 1] = start(tz.at[step], tz.at[step + 1], Z_AG + 2 * step + 1, zleft)
        elif step == 3:
            zag_r[4] = start(tz.at[5, lo], tz.at[4, lo], Z_AG + 6, zright)
            zag_l[4] = start(tz.at[3, hi], tz.at[4, hi], Z_AG + 7, zleft)

    def score_in(slot):
        s_in[:, pl.ds(slot * rows, rows)] = nt(qp[pl.ds(rows, 2 * rows), :], tz[slot])

    project(rows, rows)
    z_pass(1)
    yag_r.wait_recv()
    yag_l.wait_recv()
    yag2_r = start(ty.at[3, lo], ty.at[2, lo], Y_AG + 2, yright)
    yag2_l = start(ty.at[1, hi], ty.at[2, hi], Y_AG + 3, yleft)
    cag.append(start(ty.at[3], ty.at[7], C_AG + 1, core))
    cag.append(start(ty.at[1], ty.at[5], C_AG + 2, core))
    x1.wait_recv()
    x2.wait_recv()
    m1.wait_recv()
    m2.wait_recv()
    project(0, rows)
    project(2 * rows, rows)
    z_pass(2)
    for slot in (0, 1, 7):
        score_in(slot)
    yag2_r.wait_recv()
    yag2_l.wait_recv()
    cag.append(start(ty.at[2], ty.at[6], C_AG + 3, core))
    for one in cag:
        one.wait_recv()

    def score_hard(i):
        s_hd[:, span(i, rows)] = nt(qp[pl.ds(0, 2 * rows), :], ty[i])

    loop(2 * NY)(score_hard)

    lane = lax.broadcasted_iota(jnp.int32, (1, cols), 1)
    slot_of, row_of = lane // rows, lane % rows
    other = slot_of // NY
    owner_core = c + other - 2 * c * other
    owner = (xl * NY + lax.rem(y + slot_of % NY, NY)) * 2 + owner_core
    pairs = 2 * cols
    hard_col = (owner * pairs + blk * rows + row_of).astype(F32)
    in_col = (xh * cols + lax.rem(z * rows + lane, cols)).astype(F32)

    def stats_of(scores, out, block):
        top = jnp.max(scores, axis=1, keepdims=True)
        total = jnp.sum(jnp.exp(scores - top), axis=1, keepdims=True)
        place = lax.broadcasted_iota(jnp.int32, (scores.shape[0], 128), 1)
        out[block, :] = jnp.where(place == 0, top, total)

    def mask_hard(i):
        block = span(i, 32)
        named = meta[block, :]
        count = jnp.zeros((32, cols), F32)
        for k in range(4):
            count += jnp.where(named[:, 2 + k:3 + k] == hard_col, 1.0, 0.0)
        kept = jnp.where(count > 0.0, s_hd[block, :] + jnp.log(jnp.maximum(count, 1.0)), NEG)
        s_hd[block, :] = kept
        stats_of(kept, st_hd, block)

    z_pass(3)
    loop(2 * rows // 32)(mask_hard)
    for slot in (2, 6, 3, 5):
        score_in(slot)
    z_pass(4)
    score_in(4)

    def stats_in(i):
        block = span(i, 32)
        stats_of(s_in[block, :], st_in, block)

    loop(2 * rows // 32)(stats_in)

    a0, b0 = st_in[pl.ds(0, rows), 0:1], st_in[pl.ds(0, rows), 1:2]
    a1, b1 = st_hd[pl.ds(rows, rows), 0:1], st_hd[pl.ds(rows, rows), 1:2]
    top = jnp.maximum(a0, a1)
    total = b0 * jnp.exp(a0 - top) + b1 * jnp.exp(a1 - top)
    place = lax.broadcasted_iota(jnp.int32, (rows, 128), 1)
    packed = jnp.zeros((rows, 128), F32)
    for where, value in enumerate((
        top, total,
        st_in[pl.ds(rows, rows), 0:1], st_in[pl.ds(rows, rows), 1:2],
        st_hd[pl.ds(0, rows), 0:1], st_hd[pl.ds(0, rows), 1:2],
    )):
        packed = jnp.where(place == where, value, packed)
    stat[0] = packed
    shared = [start(stat.at[0], stat.at[d], STAT + d - 1, at(dx=d)) for d in (1, 2, 3)]
    for one in shared:
        one.wait_recv()

    def combine(parts):
        tops = [stat[d, :, w:w + 1] for d, w in parts]
        totals = [stat[d, :, w + 1:w + 2] for d, w in parts]
        top = functools.reduce(jnp.maximum, tops)
        total = sum(t * jnp.exp(m - top) for m, t in zip(tops, totals))
        return jnp.broadcast_to(top + jnp.log(total), (rows, 128))

    lse[pl.ds(0, rows), :] = combine([(0, 4), (1, 0), (3, 2)])
    lse[pl.ds(rows, rows), :] = combine([(0, 0), (1, 4), (2, 2)])
    lse[pl.ds(2 * rows, rows), :] = combine([(0, 2), (2, 0), (3, 4)])

    def grad_in(i):
        block = span(i, 32)
        wide = pl.ds(pl.multiple_of(rows + i * 32, 32), 32)
        info = meta[wide, :]
        prob = jnp.exp(s_in[block, :] - lse[wide, 0:1])
        hot = jnp.where(info[:, 1:2] == in_col, 1.0, 0.0)
        g_in[block, :] = (info[:, 0:1] * (prob - hot)).astype(BF16)

    loop(2 * rows // 32)(grad_in)

    def table_in(slot):
        return tn(g_in[:, pl.ds(slot * rows, rows)], qp[pl.ds(rows, 2 * rows), :])

    first = table_in(4).astype(BF16)
    zs[0, lo] = first[:half]
    zs[1, hi] = first[half:]
    zrs_r, zrs_l = {}, {}
    zrs_r[1] = start(zs.at[0, lo], zr.at[0, lo], Z_RS + 0, zright)
    zrs_l[1] = start(zs.at[1, hi], zr.at[1, hi], Z_RS + 1, zleft)

    def z_sum(step):
        zrs_r[step].wait_recv()
        zrs_l[step].wait_recv()
        i, j = 2 * (step - 1), 2 * step
        if step == 1:
            zs[j, lo] = (zown[0, lo] + zr[i, lo].astype(F32)).astype(BF16)
            zs[j, hi] = zown[0, hi].astype(BF16)
            zs[j + 1, lo] = zown[1, lo].astype(BF16)
            zs[j + 1, hi] = (zown[1, hi] + zr[i + 1, hi].astype(F32)).astype(BF16)
        else:
            zs[j] = (zown[2 * step - 2] + zr[i].astype(F32)).astype(BF16)
            zs[j + 1] = (zown[2 * step - 1] + zr[i + 1].astype(F32)).astype(BF16)
        zrs_r[step + 1] = start(zs.at[j], zr.at[j], Z_RS + j, zright)
        zrs_l[step + 1] = start(zs.at[j + 1], zr.at[j + 1], Z_RS + j + 1, zleft)

    zown[0] = table_in(3)
    zown[1] = table_in(5)

    def grad_hard(i):
        block = span(i, 32)
        prob = jnp.exp(s_hd[block, :] - lse[block, 0:1])
        g_hd[block, :] = (meta[block, 0:1] * prob).astype(BF16)

    loop(2 * rows // 32)(grad_hard)

    def table_hard(i):
        return tn(g_hd[:, span(i, rows)], qp[pl.ds(0, 2 * rows), :])

    def cross(i):
        cs[i] = table_hard(NY + i).astype(BF16)

    z_sum(1)

    def ahead(i):
        block = span(i, 256)
        a_in, a_hd = jnp.zeros((2 * rows, 256), F32), jnp.zeros((2 * rows, 256), F32)
        for slot in range(NZ):
            part = pl.ds(slot * rows, rows)
            a_in += nn(g_in[:, part], tz[slot, :, block])
            a_hd += nn(g_hd[:, part], ty[slot, :, block])
        at0 = 3 * rows
        xa[pl.ds(at0, rows), block] = (scale * a_hd[:rows]).astype(BF16)
        xa[pl.ds(at0 + rows, rows), block] = (scale * (a_hd[rows:] + a_in[:rows])).astype(BF16)
        xa[pl.ds(at0 + 2 * rows, rows), block] = (scale * a_in[rows:]).astype(BF16)

    loop(feat // 256)(ahead)

    def through(i):
        part = nn(xa[pl.ds(3 * rows, 3 * rows), :], head_ref[:, span(i, 256)])
        qq[lax.div(i, 2), pl.ds(0, 3 * rows), span(lax.rem(i, 2), 256)] = part.astype(BF16)
        acc[:, span(i, 256)] = part[rows:2 * rows]
        qgs[0, :, span(i, 256)] = part[:rows].astype(BF16)
        qgs[1, :, span(i, 256)] = part[2 * rows:].astype(BF16)

    loop(feat // 256)(through)
    back1 = start(qgs.at[0], qgr.at[0], X_OUT + 0, at(dx=1))
    back2 = start(qgs.at[1], qgr.at[1], X_OUT + 1, at(dx=2))

    def head_part(which):
        def one(i):
            block = span(i, 256)
            h2[which, block, :] = tn(xa[:, block], qq[which])
        loop(feat // 256)(one)

    head_part(1 - c)
    hcs[...] = h2[1 - c].astype(BF16)
    hc = start(hcs, hcr, H_C, core)
    zown[2] = table_in(2)
    zown[3] = table_in(6)
    z_sum(2)
    loop(NY)(cross)
    crs = [start(cs.at[i], cr.at[i], C_RS + i, core) for i in range(NY)]
    head_part(c)

    groups = feat // (8 * NY)
    hc.wait_recv()

    def join(i):
        block = span(i, 128)
        h2[c, block, :] = h2[c, block, :] + hcr[block, :].astype(F32)

    loop(feat // 128)(join)
    view_y = h2.at[c].reshape(groups, NY, 8, fhalf)
    hy = []
    for d in (1, 2, 3):
        there = lax.rem(y + d, NY)
        hys[d - 1] = view_y[:, there].reshape(groups * 8, fhalf).astype(BF16)
        hy.append(start(hys.at[d - 1], hyr.at[d - 1], H_Y + d - 1, at(dy=d)))

    for one in crs:
        one.wait_recv()

    def own_hard(i):
        yown[i] = table_hard(i) + cr[i].astype(F32)

    loop(NY)(own_hard)
    ys[0, lo] = yown[2, lo].astype(BF16)
    ys[1, hi] = yown[2, hi].astype(BF16)
    yrs_r = start(ys.at[0, lo], yr.at[0, lo], Y_RS + 0, yright)
    yrs_l = start(ys.at[1, hi], yr.at[1, hi], Y_RS + 1, yleft)
    zown[4] = table_in(1)
    zown[5] = table_in(7)
    z_sum(3)
    zown[6] = table_in(0)

    for one in hy:
        one.wait_recv()
    mine = view_y[:, y].reshape(groups * 8, fhalf)
    for d in range(3):
        mine = mine + hyr[d].astype(F32)
    h2[0, pl.ds(0, groups * 8), :] = mine
    view_x = h2.at[0, pl.ds(0, groups * 8)].reshape(2, NZ, 2, 8, fhalf)
    hx = []
    for d in (1, 2, 3):
        xh2 = 1 - xh if d & 2 else xh
        xl2 = 1 - xl if d & 1 else xl
        hxs[d - 1] = view_x[xh2, :, xl2].reshape(NZ * 8, fhalf).astype(BF16)
        hx.append(start(hxs.at[d - 1], hxr.at[d - 1], H_X + d - 1, at(dx=d)))

    yrs_r.wait_recv()
    yrs_l.wait_recv()
    ys[2, lo] = (yown[1, lo] + yr[0, lo].astype(F32)).astype(BF16)
    ys[2, hi] = yown[1, hi].astype(BF16)
    ys[3, lo] = yown[3, lo].astype(BF16)
    ys[3, hi] = (yown[3, hi] + yr[1, hi].astype(F32)).astype(BF16)
    yrs2_r = start(ys.at[2], yr.at[2], Y_RS + 2, yright)
    yrs2_l = start(ys.at[3], yr.at[3], Y_RS + 3, yleft)

    for one in hx:
        one.wait_recv()
    small = view_x[xh, :, xl].reshape(NZ * 8, fhalf)
    for d in range(3):
        small = small + hxr[d].astype(F32)
    hzs[...] = small.reshape(NZ, 8, fhalf)
    hz = [
        start(hzs.at[lax.rem(z + d, NZ)], hzr.at[d - 1], H_Z + d - 1, at(dz=d))
        for d in range(1, NZ)
    ]

    back1.wait_recv()
    back2.wait_recv()
    query_grad = (acc[...] + qgr[0].astype(F32) + qgr[1].astype(F32)).astype(BF16)
    qgs_own = query_grad

    def question(i):
        block = span(i, 256)
        gq_ref[:, block] = nt(qgs_own, head_ref[block, :]).astype(BF16)

    loop(feat // 256)(question)

    for one in hz:
        one.wait_recv()
    last = hzs[z]
    for d in range(NZ - 1):
        last = last + hzr[d]
    hc2s[...] = last
    hc2 = start(hc2s, hc2r, H_C2, core)

    yrs2_r.wait_recv()
    yrs2_l.wait_recv()
    zown[6] = zown[6] + yown[0] + yr[2].astype(F32) + yr[3].astype(F32)
    zrs_r[4].wait_recv()
    zrs_l[4].wait_recv()
    gt_ref[...] = (zown[6] + zr[6].astype(F32) + zr[7].astype(F32)).astype(BF16)

    hc2.wait_recv()
    theirs = hc2r[...]
    picked_own = jnp.where(c == 0, last[0:4], last[4:8])
    picked = jnp.where(c == 0, theirs[0:4], theirs[4:8])
    gh_ref[:, pl.ds(0, fhalf)] = jnp.where(c == 0, picked_own, picked)
    gh_ref[:, pl.ds(fhalf, fhalf)] = jnp.where(c == 0, picked, picked_own)

    for one in started:
        one.wait_send()


def body(q_embed, t_embed, head, positive, hard_ids, loss_weight):
    rows, feat = q_embed.shape[1:]
    cols, fhalf = NZ * rows, feat // 2
    meta = jnp.concatenate(
        [
            loss_weight[0][:, None],
            positive[0][:, None].astype(F32),
            hard_ids[0].astype(F32),
            jnp.zeros((rows, 122), F32),
        ],
        axis=1,
    )
    vmem = pl.BlockSpec(memory_space=pltpu.VMEM)
    shapes = [
        ((6 * rows, feat), BF16),
        ((2, 6 * rows, fhalf), BF16),
        ((3 * rows, feat), BF16),
        ((NZ, rows, feat), BF16),
        ((2 * NY, rows, feat), BF16),
        ((3 * rows, 128), F32),
        ((2 * rows, cols), F32),
        ((2 * rows, cols), F32),
        ((2 * rows, cols), BF16),
        ((2 * rows, cols), BF16),
        ((2 * rows, 128), F32),
        ((2 * rows, 128), F32),
        ((4, rows, 128), F32),
        ((3 * rows, 128), F32),
        ((8, rows, feat), BF16),
        ((8, rows, feat), BF16),
        ((7, rows, feat), F32),
        ((NY, rows, feat), BF16),
        ((NY, rows, feat), BF16),
        ((NY, rows, feat), F32),
        ((4, rows, feat), BF16),
        ((4, rows, feat), BF16),
        ((rows, feat), F32),
        ((2, rows, feat), BF16),
        ((2, rows, feat), BF16),
        ((2, feat, fhalf), F32),
        ((feat, fhalf), BF16),
        ((feat, fhalf), BF16),
        ((3, feat // NY, fhalf), BF16),
        ((3, feat // NY, fhalf), BF16),
        ((3, NZ * 8, fhalf), BF16),
        ((3, NZ * 8, fhalf), BF16),
        ((NZ, 8, fhalf), F32),
        ((NZ - 1, 8, fhalf), F32),
        ((8, fhalf), F32),
        ((8, fhalf), F32),
    ]
    grad_q, grad_t, grad_head = pl.pallas_call(
        kernel,
        out_shape=(
            jax.ShapeDtypeStruct((rows, feat), BF16),
            jax.ShapeDtypeStruct((rows, feat), BF16),
            jax.ShapeDtypeStruct((4, feat), F32),
        ),
        in_specs=[vmem] * 4,
        out_specs=(vmem, vmem, vmem),
        scratch_shapes=[pltpu.VMEM(s, t) for s, t in shapes] + [
            pltpu.SemaphoreType.DMA((COPIES,)),
            pltpu.SemaphoreType.DMA((COPIES,)),
        ],
        compiler_params=pltpu.CompilerParams(
            collective_id=0, has_side_effects=True, vmem_limit_bytes=56 * 1024 * 1024
        ),
    )(q_embed[0], t_embed[0], head, meta)
    return (grad_q[None], grad_t[None], grad_head)


def solution(mesh):
    in_specs = (
        P("group", "blk", None),
        P("group", "blk", None),
        P(),
        P("group", "blk"),
        P("group", "blk", None),
        P("group", "blk"),
    )
    out_specs = (P("group", "blk", None), P("group", "blk", None), P(("blk", "group"), None))
    return jax.shard_map(body, mesh=mesh, in_specs=in_specs, out_specs=out_specs, check_vma=False)
```

time: 619 us -> 106 us (0.17)
  waiting for transfers between devices: 498 us -> 0 us
  Pallas kernels: 0 us -> 97.5 us
  local copies, waits for them, and re-layouts: 39.9 us -> 6.4 us
  matrix products: 30 us -> 0 us
  starting transfers between devices: 14.8 us -> 0 us
  between operations: 14 us -> 0.65 us
  blocking collectives: 12.2 us -> 0 us
  other arithmetic: 8.13 us -> 1.4 us
    unnamed x4 -> x0, waiting for transfers between devices: 267 us -> none
    reduce_scatter x1 -> x0, waiting for transfers between devices: 145 us -> none  [body(): lax.psum_scatter((logit_scale * dot_cols(score_grad, queries)).astype(jnp...]
    pallas_call x0 -> x1, Pallas kernels: none -> 97.5 us  [body(): pl.pallas_call(kernel, out_shape=(jax.ShapeDtypeStruct((rows, feat), BF16...]
    all_to_all x2 -> x0, waiting for transfers between devices: 57.1 us -> none  [the longest x1 33.2 us: body(): lax.all_to_all(found_rows, 'group', split_axis=0, concat_axis=0, tiled=True)]
    dot_general x12 -> x0, matrix products: 30 us -> none  [the longest x3 10.9 us: dot_cols(): lax.dot_general(left, right, (((0,), (0,)), ((), ())), preferred_element_...]
    all_gather x1 -> x0, waiting for transfers between devices: 29.5 us -> none  [body(): group_keys = lax.all_gather(table_keys, 'blk', axis=0, tiled=True)]
    all_to_all x2 -> x0, starting transfers between devices: 14.3 us -> none  [the longest x1 9.29 us: body(): lax.all_to_all(outgoing.reshape(groups, capacity, feat_width), 'group', s...]
    gather x3 -> x0, local copies, waits for them, and re-layouts: 13.8 us -> none  [the longest x2 9.1 us: body(): found_rows = table_keys[incoming]]
  transfers between devices with their start and end apart: 5 -> 0, of which waited for: 5 -> 0; matrix products, arithmetic and copies ran while one was open for 9% -> 0% of each run, Pallas kernels for 0% -> 0%
where the time goes in v1:
time: 106 us
  Pallas kernels  97.5 us (92%)
  local copies, waits for them, and re-layouts  6.4 us (6%)
  other arithmetic  1.4 us (1%)
    pallas_call x1, Pallas kernels, body(): pl.pallas_call(kernel, out_shape=(jax.ShapeDtypeStruct((rows, feat), BF16...  97.5 us
    unnamed x4, local copies, waits for them, and re-layouts  5.45 us

profile of v1, /device:TPU:1, one launch (start us, length us, event | category | flops | bytes accessed | tf_op | source)
XLA Modules:
  0.0 106.0 jit_solution(11825896672387328126)
XLA Ops:
  0.6 0.7 convert_bitcast_fusion.1
  1.3 0.1 pad.3.clone
  1.4 0.1 copy.11
  1.5 0.8 copy.9
  2.3 0.8 copy.10
  3.0 0.7 maximum_maximum_fusion.meta_ref
  3.8 97.5 %shard_map.85 = (bf16[128,1024]{1,0:T(8,128)(2,1)}, bf16[128,1024]{1,0:T(8,128)(2,1)}, f32[4,1024]{1,0:T(4,128)}) custom-call(bf16[128,1024]{1,0:T(8,128)(2,1)} %bitcast.11, bf16[128,1024]{1,0:T(8,128)(2,1)} %bitcast.12, bf16[1024,1024]{1,0:T(8,128)(2,1)} %head_ref.1, f32[128,128]{1,0:T(8,128)} %maximum_maximum_fusion.meta_ref), custom_call_target="tpu_custom_call" | custom-call | tf_op jit(solution)/shard_map/pallas_call | solution.py:486
  101.3 1.7 %copy.15 = bf16[1,128,1024]{2,1,0:T(8,128)(2,1)} copy(bf16[1,128,1024]{2,1,0:T(8,128)(2,1)} %bitcast.10) | data formatting | bytes 524288
  103.0 1.7 %copy.16 = bf16[1,128,1024]{2,1,0:T(8,128)(2,1)} copy(bf16[1,128,1024]{2,1,0:T(8,128)(2,1)} %bitcast.9) | data formatting | bytes 524288
  104.7 1.3 %copy.17 = f32[4,1024]{1,0:T(4,128)} copy(f32[4,1024]{1,0:T(4,128)} %get-tuple-element.14) | data formatting | bytes 32768
  (2 shorter events, 0.0 us)

commit v2 on v1

v2 whole, which is shorter than its diff:
```python
import functools
import math

import jax
import jax.numpy as jnp
from jax import lax
from jax.experimental import pallas as pl
from jax.experimental.pallas import tpu as pltpu
from jax.sharding import PartitionSpec as P

MESH = pl.DeviceIdType.MESH
F32 = jnp.float32
BF16 = jnp.bfloat16

NZ = 8
NY = 4
NEG = -1e30


Z_AG, Y_AG, C_AG, X_IN, STAT = 0, 14, 18, 22, 26
Z_RS, C_RS, Y_RS, X_OUT = 29, 43, 47, 51
H_C, H_A1, H_B1, H_A2, H_B2, H_Z, H_C2 = 53, 54, 57, 60, 63, 66, 73
COPIES = 74


def nn(left, right):
    return lax.dot_general(left, right, (((1,), (0,)), ((), ())), preferred_element_type=F32)


def nt(left, right):
    return lax.dot_general(left, right, (((1,), (1,)), ((), ())), preferred_element_type=F32)


def tn(left, right):
    return lax.dot_general(left, right, (((0,), (0,)), ((), ())), preferred_element_type=F32)


def span(i, size):
    return pl.ds(pl.multiple_of(i * size, size), size)


def loop(count, unroll=1):
    def run(step):
        lax.fori_loop(0, count, lambda i, carry: (step(i), carry)[1], 0, unroll=unroll)
    return run


def kernel(
    qe_ref, te_ref, head_ref, weight_ref, positive_ref, ids_ref, gq_ref, gt_ref, gh_ref,
    xa, qq, qp, tz, ty, meta, info, s_in, s_hd, g_in, g_hd, st_in, st_hd, stat, wide, alpha,
    zs, zr, zown, cs, cr, yown, ys, yr, acc, qgs, qgr,
    h2, hcs, hcr, h1s, h1r, hm, h2s, h2r, hzs, hzr, hc2s, hc2r,
    send_sem, recv_sem,
):
    rows, feat = qe_ref.shape
    half = rows // 2
    scale = feat ** -0.5
    cols = NZ * rows
    fhalf, fq = feat // 2, feat // 4
    blk, grp = lax.axis_index("blk"), lax.axis_index("group")
    xh, z = lax.div(blk, NZ), lax.rem(blk, NZ)
    xl, y, c = lax.div(grp, 2 * NY), lax.rem(lax.div(grp, 2), NY), lax.rem(grp, 2)

    def at(dz=0, dy=0, dx=0, dc=0):
        xh2 = 1 - xh if dx & 2 else xh
        xl2 = 1 - xl if dx & 1 else xl
        c2 = 1 - c if dc else c
        z2, y2 = lax.rem(z + dz + NZ, NZ), lax.rem(y + dy + NY, NY)
        return (xh2 * NZ + z2, (xl2 * NY + y2) * 2 + c2)

    def copy(src, dst, sem, device):
        return pltpu.make_async_remote_copy(
            src_ref=src, dst_ref=dst, send_sem=send_sem.at[sem], recv_sem=recv_sem.at[sem],
            device_id=device, device_id_type=MESH,
        )

    peers = (
        [at(dz=d) for d in range(1, NZ)] + [at(dy=d) for d in range(1, NY)]
        + [at(dx=d) for d in (1, 2, 3)] + [at(dc=1)]
    )
    barrier = pltpu.get_barrier_semaphore()
    for peer in peers:
        pl.semaphore_signal(barrier, inc=1, device_id=peer, device_id_type=MESH)

    meta[1, 0:1, :] = weight_ref[...]
    meta[1, 1:2, :] = positive_ref[...].astype(F32)
    meta[1, 2:6, :] = ids_ref[...].astype(F32)
    meta[1, 6:8, :] = jnp.zeros((2, rows), F32)
    pl.semaphore_wait(barrier, len(peers))

    started = []

    def start(*args):
        one = copy(*args)
        one.start()
        started.append(one)
        return one

    zright, zleft = at(dz=1), at(dz=-1)
    yright, yleft = at(dy=1), at(dy=-1)
    core = at(dc=1)
    lo, hi = pl.ds(0, half), pl.ds(half, half)

    za, zb = {}, {}

    def gather_a(k):
        src = (te_ref.at[lo], te_ref.at[hi]) if k == 0 else (tz.at[NZ - k, lo], tz.at[k, hi])
        za[k] = (
            start(src[0], tz.at[NZ - 1 - k, lo], Z_AG + 2 * k, zright),
            start(src[1], tz.at[1 + k, hi], Z_AG + 2 * k + 1, zleft),
        )

    def gather_b(k):
        src = (te_ref.at[hi], te_ref.at[lo]) if k == 0 else (tz.at[NZ - k, hi], tz.at[k, lo])
        zb[k] = (
            start(src[0], tz.at[NZ - 1 - k, hi], Z_AG + 8 + 2 * k, zright),
            start(src[1], tz.at[1 + k, lo], Z_AG + 9 + 2 * k, zleft),
        )

    def arrive(pair):
        pair[0].wait_recv()
        pair[1].wait_recv()

    gather_a(0)
    m2 = start(meta.at[1], meta.at[2], X_IN + 3, at(dx=2))
    m1 = start(meta.at[1], meta.at[0], X_IN + 2, at(dx=1))
    x2 = start(qe_ref, xa.at[pl.ds(2 * rows, rows)], X_IN + 1, at(dx=2))
    x1 = start(qe_ref, xa.at[pl.ds(0, rows)], X_IN + 0, at(dx=1))
    yag = (
        start(te_ref, ty.at[3], Y_AG + 0, yright),
        start(te_ref, ty.at[1], Y_AG + 1, yleft),
    )
    gather_b(0)
    cag = [start(te_ref, ty.at[4], C_AG + 0, core)]

    tz[0] = te_ref[...]
    ty[0] = te_ref[...]
    xa[pl.ds(rows, rows), :] = qe_ref[...]

    def project(parts):
        def forward(i):
            block = span(i, 256)
            left = jnp.concatenate([xa[pl.ds(p * rows, rows), :] for p in parts], axis=0)
            out = nn(left, head_ref[:, block]).astype(BF16)
            for n, p in enumerate(parts):
                qq[lax.div(i, 2), pl.ds((3 + p) * rows, rows), span(lax.rem(i, 2), 256)] = (
                    out[n * rows:(n + 1) * rows]
                )

        loop(feat // 256)(forward)

        def back(i):
            block = span(i, 256)
            total = 0.0
            for h in range(2):
                left = jnp.concatenate(
                    [qq[h, pl.ds((3 + p) * rows, rows), :] for p in parts], axis=0
                )
                total += nt(left, head_ref[block, pl.ds(h * fhalf, fhalf)])
            out = (scale * total).astype(BF16)
            for n, p in enumerate(parts):
                qp[pl.ds(p * rows, rows), block] = out[n * rows:(n + 1) * rows]

        loop(feat // 256)(back)

    def score_in(slot):
        s_in[:, pl.ds(slot * rows, rows)] = nt(qp[pl.ds(rows, 2 * rows), :], tz[slot])

    project([1])
    arrive(za[0])
    gather_a(1)
    arrive(yag)
    yag2 = (
        start(ty.at[3, lo], ty.at[2, lo], Y_AG + 2, yright),
        start(ty.at[1, hi], ty.at[2, hi], Y_AG + 3, yleft),
    )
    cag.append(start(ty.at[3], ty.at[7], C_AG + 1, core))
    cag.append(start(ty.at[1], ty.at[5], C_AG + 2, core))
    arrive(zb[0])
    gather_b(1)
    arrive(za[1])
    gather_a(2)
    arrive(yag2)
    cag.append(start(ty.at[2], ty.at[6], C_AG + 3, core))
    arrive(zb[1])
    gather_b(2)
    for one in (m1, m2, x1, x2):
        one.wait_recv()
    project([0, 2])
    arrive(za[2])
    gather_a(3)

    for p in range(3):
        wide[pl.ds(0, 8), :] = meta[p]
        info[pl.ds(p * rows, rows), :] = jnp.transpose(wide[...])
    for one in cag:
        one.wait_recv()

    def score_hard(i):
        s_hd[:, span(i, rows)] = nt(qp[pl.ds(0, 2 * rows), :], ty[i])

    loop(2 * NY)(score_hard)

    lane = lax.broadcasted_iota(jnp.int32, (1, cols), 1)
    slot_of, row_of = lane // rows, lane % rows
    other = slot_of // NY
    owner_core = c + other - 2 * c * other
    owner = (xl * NY + lax.rem(y + slot_of % NY, NY)) * 2 + owner_core
    hard_col = (owner * (2 * cols) + blk * rows + row_of).astype(F32)
    in_col = (xh * cols + lax.rem(z * rows + lane, cols)).astype(F32)

    def two_lanes(first, second):
        place = lax.broadcasted_iota(jnp.int32, (first.shape[0], 128), 1)
        return jnp.where(place == 0, first, second)

    def mask_hard(i):
        block = span(i, 32)
        named = info[block, :]
        count = jnp.zeros((32, cols), F32)
        for k in range(4):
            count += jnp.where(named[:, 2 + k:3 + k] == hard_col, 1.0, 0.0)
        kept = jnp.where(count > 0.0, s_hd[block, :] + jnp.log(jnp.maximum(count, 1.0)), NEG)
        top = jnp.max(kept, axis=1, keepdims=True)
        prob = jnp.exp(kept - top)
        s_hd[block, :] = prob
        st_hd[block, :] = two_lanes(top, jnp.sum(prob, axis=1, keepdims=True))

    loop(2 * rows // 32)(mask_hard)
    for slot in (0, 7, 1, 6, 2):
        score_in(slot)
    arrive(zb[2])
    for slot in (5, 3):
        score_in(slot)

    left, right = pl.ds(0, 4 * rows), pl.ds(5 * rows, 3 * rows)
    last_cols = pl.ds(4 * rows, rows)

    def stats_most(i):
        block = span(i, 32)
        one, two = s_in[block, left], s_in[block, right]
        top = jnp.maximum(
            jnp.max(one, axis=1, keepdims=True), jnp.max(two, axis=1, keepdims=True)
        )
        one, two = jnp.exp(one - top), jnp.exp(two - top)
        s_in[block, left] = one
        s_in[block, right] = two
        total = jnp.sum(one, axis=1, keepdims=True) + jnp.sum(two, axis=1, keepdims=True)
        st_in[block, pl.ds(0, 128)] = two_lanes(top, total)

    loop(2 * rows // 32)(stats_most)
    arrive(za[3])
    score_in(4)
    scores = s_in[:, last_cols]
    top = jnp.max(scores, axis=1, keepdims=True)
    prob = jnp.exp(scores - top)
    s_in[:, last_cols] = prob
    st_in[:, pl.ds(128, 128)] = two_lanes(top, jnp.sum(prob, axis=1, keepdims=True))

    place = lax.broadcasted_iota(jnp.int32, (rows, 128), 1)
    own, partner = pl.ds(0, rows), pl.ds(rows, rows)
    packed = jnp.zeros((rows, 128), F32)
    for where, value in enumerate((
        st_in[own, 0:1], st_in[own, 1:2], st_in[own, 128:129], st_in[own, 129:130],
        st_in[partner, 0:1], st_in[partner, 1:2], st_in[partner, 128:129], st_in[partner, 129:130],
        st_hd[partner, 0:1], st_hd[partner, 1:2], st_hd[own, 0:1], st_hd[own, 1:2],
    )):
        packed = jnp.where(place == where, value, packed)
    wide[...] = jnp.transpose(packed)

    def merge(parts):
        top = functools.reduce(jnp.maximum, [m for m, _ in parts])
        return top, sum(t * jnp.exp(m - top) for m, t in parts)

    def pair(ref, n):
        return ref[2 * n:2 * n + 1, :], ref[2 * n + 1:2 * n + 2, :]

    mine = merge([pair(wide, 0), pair(wide, 1), pair(wide, 4)])
    theirs = merge([pair(wide, 2), pair(wide, 3)])
    stat[0, 0:1, :], stat[0, 1:2, :] = mine
    stat[0, 2:3, :], stat[0, 3:4, :] = theirs
    stat[0, 4:6, :] = wide[10:12, :]
    stat[0, 6:8, :] = jnp.zeros((2, rows), F32)
    shared = [start(stat.at[0], stat.at[d], STAT + d - 1, at(dx=d)) for d in (1, 2, 3)]
    for one in shared:
        one.wait_recv()

    def log_total(parts):
        top, total = merge([pair(stat.at[d], n) for d, n in parts])
        return top + jnp.log(total)

    lse = [
        log_total([(0, 2), (1, 0), (3, 1)]),
        log_total([(0, 0), (1, 2), (2, 1)]),
        log_total([(0, 1), (2, 0), (3, 2)]),
    ]

    def factor(p, row):
        return meta[p, 0:1, :] * jnp.exp(wide[row:row + 1, :] - lse[p])

    factors = [
        factor(1, 0), factor(1, 2), factor(2, 4), factor(2, 6), factor(1, 8), factor(0, 10),
    ]
    for n, value in enumerate(factors):
        wide[n:n + 1, :] = value
    alpha[...] = jnp.transpose(wide[...])

    def grad_last(n):
        block = pl.ds(n * rows, rows)
        facts = info[pl.ds((1 + n) * rows, rows), :]
        hot = jnp.where(facts[:, 1:2] == in_col[:, 4 * rows:5 * rows], facts[:, 0:1], 0.0)
        a = alpha[:, 2 * n + 1:2 * n + 2]
        g_in[block, last_cols] = (a * s_in[block, last_cols] - hot).astype(BF16)

    grad_last(0)
    grad_last(1)

    def table_in(slot):
        return tn(g_in[:, pl.ds(slot * rows, rows)], qp[pl.ds(rows, 2 * rows), :])

    def table_pair(slot):
        both = tn(g_in[:, pl.ds(slot * rows, 2 * rows)], qp[pl.ds(rows, 2 * rows), :])
        zown[slot] = both[:rows]
        zown[slot + 1] = both[rows:]

    first = table_in(4).astype(BF16)
    zs[0, lo] = first[:half]
    zs[4, hi] = first[half:]
    ra, rb = {}, {}

    def reduce_a(k):
        ra[k] = (
            start(zs.at[k, lo], zr.at[k, lo], Z_RS + 2 * k, zright),
            start(zs.at[4 + k, hi], zr.at[4 + k, hi], Z_RS + 2 * k + 1, zleft),
        )

    def reduce_b(k):
        rb[k] = (
            start(zs.at[k, hi], zr.at[k, hi], Z_RS + 6 + 2 * k, zright),
            start(zs.at[4 + k, lo], zr.at[4 + k, lo], Z_RS + 7 + 2 * k, zleft),
        )

    def sum_a(k):
        arrive(ra[k])
        zs[k + 1, lo] = (zown[3 - k, lo] + zr[k, lo].astype(F32)).astype(BF16)
        zs[5 + k, hi] = (zown[5 + k, hi] + zr[4 + k, hi].astype(F32)).astype(BF16)
        reduce_a(k + 1)

    def sum_b(k):
        arrive(rb[k])
        zs[k + 1, hi] = (zown[3 - k, hi] + zr[k, hi].astype(F32)).astype(BF16)
        zs[5 + k, lo] = (zown[5 + k, lo] + zr[4 + k, lo].astype(F32)).astype(BF16)
        reduce_b(k + 1)

    reduce_a(0)

    def grad_most(n):
        def one(i):
            block = span(i, 32)
            low = pl.ds(pl.multiple_of(n * rows + i * 32, 32), 32)
            facts = info[pl.ds(pl.multiple_of((1 + n) * rows + i * 32, 32), 32), :]
            a, w, target = alpha[block, 2 * n:2 * n + 1], facts[:, 0:1], facts[:, 1:2]
            for part, begin, size in ((left, 0, 4 * rows), (right, 5 * rows, 3 * rows)):
                hot = jnp.where(target == in_col[:, begin:begin + size], w, 0.0)
                g_in[low, part] = (a * s_in[low, part] - hot).astype(BF16)

        loop(rows // 32)(one)

    grad_most(0)
    grad_most(1)

    def grad_hard(i):
        block = span(i, 32)
        g_hd[block, :] = (alpha[block, 5:6] * s_hd[block, :]).astype(BF16)
        low = pl.ds(pl.multiple_of(rows + i * 32, 32), 32)
        g_hd[low, :] = (alpha[block, 4:5] * s_hd[low, :]).astype(BF16)

    loop(rows // 32)(grad_hard)

    table_pair(2)
    table_pair(5)
    zs[1, hi] = zown[3, hi].astype(BF16)
    zs[5, lo] = zown[5, lo].astype(BF16)
    reduce_b(1)

    def ahead(i):
        block = span(i, 256)
        a_in, a_hd = jnp.zeros((2 * rows, 256), F32), jnp.zeros((2 * rows, 256), F32)
        for n in range(NZ // 2):
            part, two = pl.ds(2 * n * rows, 2 * rows), pl.ds(2 * n, 2)
            a_in += nn(g_in[:, part], tz[two, :, block].reshape(2 * rows, 256))
            a_hd += nn(g_hd[:, part], ty[two, :, block].reshape(2 * rows, 256))
        at0 = 3 * rows
        xa[pl.ds(at0, rows), block] = (scale * a_hd[:rows]).astype(BF16)
        xa[pl.ds(at0 + rows, rows), block] = (scale * (a_hd[rows:] + a_in[:rows])).astype(BF16)
        xa[pl.ds(at0 + 2 * rows, rows), block] = (scale * a_in[rows:]).astype(BF16)

    loop(feat // 256)(ahead)
    sum_a(0)

    def through(i):
        part = nn(xa[pl.ds(3 * rows, 3 * rows), :], head_ref[:, span(i, 256)])
        qq[lax.div(i, 2), pl.ds(0, 3 * rows), span(lax.rem(i, 2), 256)] = part.astype(BF16)
        acc[:, span(i, 256)] = part[rows:2 * rows]
        qgs[0, :, span(i, 256)] = part[:rows].astype(BF16)
        qgs[1, :, span(i, 256)] = part[2 * rows:].astype(BF16)

    loop(feat // 256)(through)
    back = (
        start(qgs.at[0], qgr.at[0], X_OUT + 0, at(dx=1)),
        start(qgs.at[1], qgr.at[1], X_OUT + 1, at(dx=2)),
    )
    sum_b(1)
    def head_part(which, out):
        def one(i):
            block = span(i, 256)
            out(block, tn(xa[:, block], qq[which]))
        loop(feat // 256)(one)

    def give(block, value):
        hcs[block, :] = value.astype(BF16)

    head_part(1 - c, give)
    hc = start(hcs, hcr, H_C, core)
    sum_a(1)

    def keep(block, value):
        h2[block, :] = value

    head_part(c, keep)
    zown[7] = table_in(7)
    table_pair(0)
    sum_b(2)
    hc.wait_recv()

    def join(i):
        block = span(i, 128)
        h2[block, :] = h2[block, :] + hcr[block, :].astype(F32)

    loop(feat // 128)(join)

    groups = feat // (8 * NY)
    view_a = h2.reshape(groups, NY, 8, fhalf)
    view_b = h2.reshape(2, NZ, 2, 8 * NY, fhalf)

    def cross_x(d):
        return (1 - xh if d & 2 else xh), (1 - xl if d & 1 else xl)

    stage1 = []
    for d in (1, 2, 3):
        there = lax.rem(y + d, NY)
        h1s[d - 1] = view_a[:, there, :, 0:fq].reshape(groups * 8, fq).astype(BF16)
        stage1.append(start(h1s.at[d - 1], h1r.at[d - 1], H_A1 + d - 1, at(dy=d)))
        xh2, xl2 = cross_x(d)
        h1s[d + 2] = view_b[xh2, :, xl2, :, fq:fhalf].reshape(groups * 8, fq).astype(BF16)
        stage1.append(start(h1s.at[d + 2], h1r.at[d + 2], H_B1 + d - 1, at(dx=d)))
    sum_a(2)

    def table_hard(i):
        return tn(g_hd[:, span(i, rows)], qp[pl.ds(0, 2 * rows), :])

    def cross(i):
        cs[i] = table_hard(NY + i).astype(BF16)

    loop(NY)(cross)
    crs = [start(cs.at[i], cr.at[i], C_RS + i, core) for i in range(NY)]
    for one in crs:
        one.wait_recv()

    def own_hard(i):
        yown[i] = table_hard(i) + cr[i].astype(F32)

    loop(NY)(own_hard)
    ys[0, lo] = yown[2, lo].astype(BF16)
    ys[1, hi] = yown[2, hi].astype(BF16)
    yrs = (
        start(ys.at[0, lo], yr.at[0, lo], Y_RS + 0, yright),
        start(ys.at[1, hi], yr.at[1, hi], Y_RS + 1, yleft),
    )

    hm[0] = view_a[:, y, :, 0:fq].reshape(groups * 8, fq)
    hm[1] = view_b[xh, :, xl, :, fq:fhalf].reshape(groups * 8, fq)
    for one in stage1:
        one.wait_recv()
    for n in range(2):
        hm[n] = (hm[n] + h1r[3 * n].astype(F32)) + (
            h1r[3 * n + 1].astype(F32) + h1r[3 * n + 2].astype(F32)
        )
    part_a = hm.at[0].reshape(2, NZ, 2, 8, fq)
    part_b = hm.at[1].reshape(NZ, NY, 8, fq)
    stage2 = []
    for d in (1, 2, 3):
        xh2, xl2 = cross_x(d)
        h2s[d - 1] = part_a[xh2, :, xl2].reshape(NZ * 8, fq).astype(BF16)
        stage2.append(start(h2s.at[d - 1], h2r.at[d - 1], H_A2 + d - 1, at(dx=d)))
        there = lax.rem(y + d, NY)
        h2s[d + 2] = part_b[:, there].reshape(NZ * 8, fq).astype(BF16)
        stage2.append(start(h2s.at[d + 2], h2r.at[d + 2], H_B2 + d - 1, at(dy=d)))
    arrive(yrs)
    ys[2, lo] = (yown[1, lo] + yr[0, lo].astype(F32)).astype(BF16)
    ys[2, hi] = yown[1, hi].astype(BF16)
    ys[3, lo] = yown[3, lo].astype(BF16)
    ys[3, hi] = (yown[3, hi] + yr[1, hi].astype(F32)).astype(BF16)
    yrs2 = (
        start(ys.at[2], yr.at[2], Y_RS + 2, yright),
        start(ys.at[3], yr.at[3], Y_RS + 3, yleft),
    )

    arrive(rb[3])
    for one in stage2:
        one.wait_recv()
    small_a = part_a[xh, :, xl].reshape(NZ * 8, fq)
    small_b = part_b[:, y].reshape(NZ * 8, fq)
    for d in range(3):
        small_a = small_a + h2r[d].astype(F32)
        small_b = small_b + h2r[d + 3].astype(F32)
    hzs[:, :, pl.ds(0, fq)] = small_a.reshape(NZ, 8, fq)
    hzs[:, :, pl.ds(fq, fq)] = small_b.reshape(NZ, 8, fq)
    hz = [
        start(hzs.at[lax.rem(z + d, NZ)], hzr.at[d - 1], H_Z + d - 1, at(dz=d))
        for d in range(1, NZ)
    ]

    arrive(back)
    acc[...] = acc[...] + qgr[0].astype(F32) + qgr[1].astype(F32)

    def question(i):
        block = span(i, 256)
        gq_ref[:, block] = nt(acc[...].astype(BF16), head_ref[block, :]).astype(BF16)

    loop(feat // 256)(question)

    for one in hz:
        one.wait_recv()
    last = hzs[z]
    for d in range(NZ - 1):
        last = last + hzr[d]
    hc2s[...] = last
    hc2 = start(hc2s, hc2r, H_C2, core)

    arrive(yrs2)
    zown[0] = (zown[0] + yown[0]) + (yr[2].astype(F32) + yr[3].astype(F32))
    arrive(ra[3])
    gt_ref[...] = (zown[0] + (zr[3].astype(F32) + zr[7].astype(F32))).astype(BF16)

    hc2.wait_recv()
    far = hc2r[...]
    picked_own = jnp.where(c == 0, last[0:4], last[4:8])
    picked = jnp.where(c == 0, far[0:4], far[4:8])
    gh_ref[:, pl.ds(0, fhalf)] = jnp.where(c == 0, picked_own, picked)
    gh_ref[:, pl.ds(fhalf, fhalf)] = jnp.where(c == 0, picked, picked_own)

    for one in started:
        one.wait_send()


def hand_over(*refs):
    for source, target in zip(refs[:3], refs[3:]):
        target[...] = source[...]


def body(q_embed, t_embed, head, positive, hard_ids, loss_weight):
    rows, feat = q_embed.shape[1:]
    cols, fhalf, fq = NZ * rows, feat // 2, feat // 4
    vmem = pl.BlockSpec(memory_space=pltpu.VMEM)
    shapes = [
        ((6 * rows, feat), BF16),
        ((2, 6 * rows, fhalf), BF16),
        ((3 * rows, feat), BF16),
        ((NZ, rows, feat), BF16),
        ((2 * NY, rows, feat), BF16),
        ((3, 8, rows), F32),
        ((3 * rows, 128), F32),
        ((2 * rows, cols), F32),
        ((2 * rows, cols), F32),
        ((2 * rows, cols), BF16),
        ((2 * rows, cols), BF16),
        ((2 * rows, 256), F32),
        ((2 * rows, 128), F32),
        ((4, 8, rows), F32),
        ((128, rows), F32),
        ((rows, 128), F32),
        ((8, rows, feat), BF16),
        ((8, rows, feat), BF16),
        ((8, rows, feat), F32),
        ((NY, rows, feat), BF16),
        ((NY, rows, feat), BF16),
        ((NY, rows, feat), F32),
        ((4, rows, feat), BF16),
        ((4, rows, feat), BF16),
        ((rows, feat), F32),
        ((2, rows, feat), BF16),
        ((2, rows, feat), BF16),
        ((feat, fhalf), F32),
        ((feat, fhalf), BF16),
        ((feat, fhalf), BF16),
        ((6, feat // NY, fq), BF16),
        ((6, feat // NY, fq), BF16),
        ((2, feat // NY, fq), F32),
        ((6, NZ * 8, fq), BF16),
        ((6, NZ * 8, fq), BF16),
        ((NZ, 8, fhalf), F32),
        ((NZ - 1, 8, fhalf), F32),
        ((8, fhalf), F32),
        ((8, fhalf), F32),
    ]
    outs = (
        jax.ShapeDtypeStruct((rows, feat), BF16),
        jax.ShapeDtypeStruct((rows, feat), BF16),
        jax.ShapeDtypeStruct((4, feat), F32),
    )
    results = pl.pallas_call(
        kernel,
        out_shape=outs,
        in_specs=[vmem] * 6,
        out_specs=(vmem, vmem, vmem),
        scratch_shapes=[pltpu.VMEM(s, t) for s, t in shapes] + [
            pltpu.SemaphoreType.DMA((COPIES,)),
            pltpu.SemaphoreType.DMA((COPIES,)),
        ],
        compiler_params=pltpu.CompilerParams(
            collective_id=0, has_side_effects=True, vmem_limit_bytes=56 * 1024 * 1024
        ),
    )(q_embed[0], t_embed[0], head, loss_weight, positive, hard_ids[0].T)
    grad_q, grad_t, grad_head = pl.pallas_call(
        hand_over,
        out_shape=outs,
        in_specs=[vmem] * 3,
        out_specs=(vmem, vmem, vmem),
    )(*results)
    return (grad_q[None], grad_t[None], grad_head)


def solution(mesh):
    in_specs = (
        P("group", "blk", None),
        P("group", "blk", None),
        P(),
        P("group", "blk"),
        P("group", "blk", None),
        P("group", "blk"),
    )
    out_specs = (P("group", "blk", None), P("group", "blk", None), P(("blk", "group"), None))
    return jax.shard_map(body, mesh=mesh, in_specs=in_specs, out_specs=out_specs, check_vma=False)
```

time: 106 us -> 81.2 us (0.77)
  Pallas kernels: 97.5 us -> 80.4 us
  local copies, waits for them, and re-layouts: 6.4 us -> 0 us
  other arithmetic: 1.4 us -> 0 us
    pallas_call x1 -> x2, Pallas kernels: 97.5 us -> 80.4 us  [the longest x1 78.5 us: body(): pl.pallas_call(kernel, out_shape=outs, in_specs=[vmem] * 6, out_specs=(vm...]
    unnamed x4 -> x0, local copies, waits for them, and re-layouts: 5.45 us -> none
where the time goes in v2:
time: 81.2 us; the launch traced here: 81 us
  Pallas kernels  80.4 us (99%)
    pallas_call x1, Pallas kernels, body(): pl.pallas_call(kernel, out_shape=outs, in_specs=[vmem] * 6, out_specs=(vm...  78.5 us
    pallas_call x1, Pallas kernels, body(): pl.pallas_call(hand_over, out_shape=outs, in_specs=[vmem] * 3, out_specs=...  1.84 us

profile of v2, /device:TPU:1, one launch (start us, length us, event | category | flops | bytes accessed | tf_op | source)
XLA Modules:
  0.0 81.0 jit_solution(15864603906181336930)
XLA Ops:
  0.6 78.5 %shard_map.85 = (bf16[128,1024]{1,0:T(8,128)(2,1)}, bf16[128,1024]{1,0:T(8,128)(2,1)}, f32[4,1024]{1,0:T(4,128)}) custom-call(bf16[128,1024]{1,0:T(8,128)(2,1)} %bitcast.7, bf16[128,1024]{1,0:T(8,128)(2,1)} %bitcast.8, bf16[1024,1024]{1,0:T(8,128)(2,1)} %head_ref.1, f32[1,128]{1,0:T(1,128)} %weight_ref.1, s32[1,128]{1,0:T(1,128)} %positive_ref.1, ...), custom_call_target="tpu_custom_call" | custom-call | tf_op jit(solution)/shard_map/pallas_call | solution.py:611
  79.2 1.8 %shard_map.86 = (bf16[128,1024]{1,0:T(8,128)(2,1)}, bf16[128,1024]{1,0:T(8,128)(2,1)}, f32[4,1024]{1,0:T(4,128)}) custom-call(bf16[128,1024]{1,0:T(8,128)(2,1)} %get-tuple-element.9.refs_0_, bf16[128,1024]{1,0:T(8,128)(2,1)} %get-tuple-element.10.refs_1_, f32[4,1024]{1,0:T(4,128)} %get-tuple-element.11.refs_2_), custom_call_target="tpu_custom_call" | custom-call | tf_op jit(solution)/shard_map/pallas_call | solution.py:624

commit v3 on v2

--- a/solution.py
+++ b/solution.py
@@ -19,8 +19,8 @@
 
 Z_AG, Y_AG, C_AG, X_IN, STAT = 0, 14, 18, 22, 26
 Z_RS, C_RS, Y_RS, X_OUT = 29, 43, 47, 51
-H_C, H_A1, H_B1, H_A2, H_B2, H_Z, H_C2 = 53, 54, 57, 60, 63, 66, 73
-COPIES = 74
+H_IN, H_A1, H_B1, H_A2, H_B2, H_Z = 53, 57, 60, 63, 66, 69
+COPIES = 84
 
 
 def nn(left, right):
@@ -48,8 +48,8 @@
 def kernel(
     qe_ref, te_ref, head_ref, weight_ref, positive_ref, ids_ref, gq_ref, gt_ref, gh_ref,
     xa, qq, qp, tz, ty, meta, info, s_in, s_hd, g_in, g_hd, st_in, st_hd, stat, wide, alpha,
-    zs, zr, zown, cs, cr, yown, ys, yr, acc, qgs, qgr,
-    h2, hcs, hcr, h1s, h1r, hm, h2s, h2r, hzs, hzr, hc2s, hc2r,
+    zs, zr, zown, cs, cr, yown, ys, yr, acc, ar,
+    h2, xap, qqp, h1s, h1r, hm, h2s, h2r, hzs, hzr,
     send_sem, recv_sem,
 ):
     rows, feat = qe_ref.shape
@@ -75,7 +75,7 @@
         )
 
     peers = (
-        [at(dz=d) for d in range(1, NZ)] + [at(dy=d) for d in range(1, NY)]
+        [at(dz=d) for d in (1, -1)] + [at(dy=d) for d in (1, -1)]
         + [at(dx=d) for d in (1, 2, 3)] + [at(dc=1)]
     )
     barrier = pltpu.get_barrier_semaphore()
@@ -138,7 +138,7 @@
     xa[pl.ds(rows, rows), :] = qe_ref[...]
 
     def project(parts):
-        def forward(i):
+        def one(i):
             block = span(i, 256)
             left = jnp.concatenate([xa[pl.ds(p * rows, rows), :] for p in parts], axis=0)
             out = nn(left, head_ref[:, block]).astype(BF16)
@@ -147,9 +147,10 @@
                     out[n * rows:(n + 1) * rows]
                 )
 
-        loop(feat // 256)(forward)
-
-        def back(i):
+        loop(feat // 256)(one)
+
+    def project_back(parts):
+        def one(i):
             block = span(i, 256)
             total = 0.0
             for h in range(2):
@@ -161,45 +162,20 @@
             for n, p in enumerate(parts):
                 qp[pl.ds(p * rows, rows), block] = out[n * rows:(n + 1) * rows]
 
-        loop(feat // 256)(back)
-
-    def score_in(slot):
-        s_in[:, pl.ds(slot * rows, rows)] = nt(qp[pl.ds(rows, 2 * rows), :], tz[slot])
+        loop(feat // 256)(one)
+
+    low, high, top_rows = pl.ds(0, rows), pl.ds(rows, rows), pl.ds(2 * rows, rows)
+
+    def score_in(slot, where, what):
+        s_in[where, pl.ds(slot * rows, rows)] = nt(qp[what, :], tz[slot])
 
     project([1])
-    arrive(za[0])
-    gather_a(1)
-    arrive(yag)
-    yag2 = (
-        start(ty.at[3, lo], ty.at[2, lo], Y_AG + 2, yright),
-        start(ty.at[1, hi], ty.at[2, hi], Y_AG + 3, yleft),
-    )
-    cag.append(start(ty.at[3], ty.at[7], C_AG + 1, core))
-    cag.append(start(ty.at[1], ty.at[5], C_AG + 2, core))
-    arrive(zb[0])
-    gather_b(1)
-    arrive(za[1])
-    gather_a(2)
-    arrive(yag2)
-    cag.append(start(ty.at[2], ty.at[6], C_AG + 3, core))
-    arrive(zb[1])
-    gather_b(2)
-    for one in (m1, m2, x1, x2):
-        one.wait_recv()
-    project([0, 2])
-    arrive(za[2])
-    gather_a(3)
-
+    project_back([1])
+    m1.wait_recv()
+    m2.wait_recv()
     for p in range(3):
         wide[pl.ds(0, 8), :] = meta[p]
         info[pl.ds(p * rows, rows), :] = jnp.transpose(wide[...])
-    for one in cag:
-        one.wait_recv()
-
-    def score_hard(i):
-        s_hd[:, span(i, rows)] = nt(qp[pl.ds(0, 2 * rows), :], ty[i])
-
-    loop(2 * NY)(score_hard)
 
     lane = lax.broadcasted_iota(jnp.int32, (1, cols), 1)
     slot_of, row_of = lane // rows, lane % rows
@@ -209,28 +185,74 @@
     hard_col = (owner * (2 * cols) + blk * rows + row_of).astype(F32)
     in_col = (xh * cols + lax.rem(z * rows + lane, cols)).astype(F32)
 
-    def two_lanes(first, second):
-        place = lax.broadcasted_iota(jnp.int32, (first.shape[0], 128), 1)
-        return jnp.where(place == 0, first, second)
-
     def mask_hard(i):
         block = span(i, 32)
         named = info[block, :]
         count = jnp.zeros((32, cols), F32)
         for k in range(4):
             count += jnp.where(named[:, 2 + k:3 + k] == hard_col, 1.0, 0.0)
-        kept = jnp.where(count > 0.0, s_hd[block, :] + jnp.log(jnp.maximum(count, 1.0)), NEG)
+        s_hd[block, :] = jnp.where(count > 0.0, jnp.log(jnp.maximum(count, 1.0)), NEG)
+
+    arrive(za[0])
+    gather_a(1)
+    loop(rows // 32)(mask_hard)
+    arrive(zb[0])
+    gather_b(1)
+    arrive(yag)
+    yag2 = (
+        start(ty.at[3, lo], ty.at[2, lo], Y_AG + 2, yright),
+        start(ty.at[1, hi], ty.at[2, hi], Y_AG + 3, yleft),
+    )
+    cag.append(start(ty.at[3], ty.at[7], C_AG + 1, core))
+    cag.append(start(ty.at[1], ty.at[5], C_AG + 2, core))
+    loop(rows // 32)(lambda i: mask_hard(i + rows // 32))
+    arrive(za[1])
+    gather_a(2)
+    arrive(yag2)
+    cag.append(start(ty.at[2], ty.at[6], C_AG + 3, core))
+    arrive(zb[1])
+    gather_b(2)
+
+    def score_hard(where):
+        def one(i):
+            block = span(i, rows)
+            s_hd[where, block] = s_hd[where, block] + nt(qp[where, :], ty[i])
+        loop(2 * NY)(one)
+
+    def two_lanes(first, second):
+        place = lax.broadcasted_iota(jnp.int32, (first.shape[0], 128), 1)
+        return jnp.where(place == 0, first, second)
+
+    def stats_hard(i):
+        block = span(i, 32)
+        kept = s_hd[block, :]
         top = jnp.max(kept, axis=1, keepdims=True)
         prob = jnp.exp(kept - top)
         s_hd[block, :] = prob
         st_hd[block, :] = two_lanes(top, jnp.sum(prob, axis=1, keepdims=True))
 
-    loop(2 * rows // 32)(mask_hard)
+    for one in cag:
+        one.wait_recv()
+    arrive(za[2])
+    gather_a(3)
+    score_hard(high)
+    loop(rows // 32)(lambda i: stats_hard(i + rows // 32))
     for slot in (0, 7, 1, 6, 2):
-        score_in(slot)
+        score_in(slot, low, high)
+    x1.wait_recv()
+    x2.wait_recv()
+    early, late = pl.ds(0, 3 * rows), pl.ds(3 * rows, 3 * rows)
+    operands = [start(xa.at[early], xap.at[early], H_IN + 0, core)]
+    project([0, 2])
+    operands.append(start(qq.at[1 - c, late], qqp.at[late], H_IN + 1, core))
+    project_back([0, 2])
+    score_hard(low)
+    loop(rows // 32)(stats_hard)
+    for slot in (0, 7, 1, 6, 2):
+        score_in(slot, high, top_rows)
     arrive(zb[2])
     for slot in (5, 3):
-        score_in(slot)
+        score_in(slot, pl.ds(0, 2 * rows), pl.ds(rows, 2 * rows))
 
     left, right = pl.ds(0, 4 * rows), pl.ds(5 * rows, 3 * rows)
     last_cols = pl.ds(4 * rows, rows)
@@ -249,7 +271,7 @@
 
     loop(2 * rows // 32)(stats_most)
     arrive(za[3])
-    score_in(4)
+    score_in(4, pl.ds(0, 2 * rows), pl.ds(rows, 2 * rows))
     scores = s_in[:, last_cols]
     top = jnp.max(scores, axis=1, keepdims=True)
     prob = jnp.exp(scores - top)
@@ -356,12 +378,12 @@
     def grad_most(n):
         def one(i):
             block = span(i, 32)
-            low = pl.ds(pl.multiple_of(n * rows + i * 32, 32), 32)
+            place = pl.ds(pl.multiple_of(n * rows + i * 32, 32), 32)
             facts = info[pl.ds(pl.multiple_of((1 + n) * rows + i * 32, 32), 32), :]
             a, w, target = alpha[block, 2 * n:2 * n + 1], facts[:, 0:1], facts[:, 1:2]
             for part, begin, size in ((left, 0, 4 * rows), (right, 5 * rows, 3 * rows)):
                 hot = jnp.where(target == in_col[:, begin:begin + size], w, 0.0)
-                g_in[low, part] = (a * s_in[low, part] - hot).astype(BF16)
+                g_in[place, part] = (a * s_in[place, part] - hot).astype(BF16)
 
         loop(rows // 32)(one)
 
@@ -371,8 +393,8 @@
     def grad_hard(i):
         block = span(i, 32)
         g_hd[block, :] = (alpha[block, 5:6] * s_hd[block, :]).astype(BF16)
-        low = pl.ds(pl.multiple_of(rows + i * 32, 32), 32)
-        g_hd[low, :] = (alpha[block, 4:5] * s_hd[low, :]).astype(BF16)
+        place = pl.ds(pl.multiple_of(rows + i * 32, 32), 32)
+        g_hd[place, :] = (alpha[block, 4:5] * s_hd[place, :]).astype(BF16)
 
     loop(rows // 32)(grad_hard)
 
@@ -381,6 +403,13 @@
     zs[1, hi] = zown[3, hi].astype(BF16)
     zs[5, lo] = zown[5, lo].astype(BF16)
     reduce_b(1)
+
+    def table_hard(first):
+        many = tn(g_hd[:, pl.ds(first * rows, NY * rows)], qp[pl.ds(0, 2 * rows), :])
+        return many.reshape(NY, rows, feat)
+
+    cs[...] = table_hard(NY).astype(BF16)
+    cross = start(cs, cr, C_RS, core)
 
     def ahead(i):
         block = span(i, 256)
@@ -391,52 +420,43 @@
             a_hd += nn(g_hd[:, part], ty[two, :, block].reshape(2 * rows, 256))
         at0 = 3 * rows
         xa[pl.ds(at0, rows), block] = (scale * a_hd[:rows]).astype(BF16)
-        xa[pl.ds(at0 + rows, rows), block] = (scale * (a_hd[rows:] + a_in[:rows])).astype(BF16)
+        own_part = scale * (a_hd[rows:] + a_in[:rows])
+        acc[:, block] = own_part
+        xa[pl.ds(at0 + rows, rows), block] = own_part.astype(BF16)
         xa[pl.ds(at0 + 2 * rows, rows), block] = (scale * a_in[rows:]).astype(BF16)
 
     loop(feat // 256)(ahead)
-    sum_a(0)
-
+    back = (
+        start(xa.at[pl.ds(3 * rows, rows)], ar.at[0], X_OUT + 0, at(dx=1)),
+        start(xa.at[pl.ds(5 * rows, rows)], ar.at[1], X_OUT + 1, at(dx=2)),
+    )
+    operands.append(start(xa.at[late], xap.at[late], H_IN + 2, core))
     def through(i):
         part = nn(xa[pl.ds(3 * rows, 3 * rows), :], head_ref[:, span(i, 256)])
         qq[lax.div(i, 2), pl.ds(0, 3 * rows), span(lax.rem(i, 2), 256)] = part.astype(BF16)
-        acc[:, span(i, 256)] = part[rows:2 * rows]
-        qgs[0, :, span(i, 256)] = part[:rows].astype(BF16)
-        qgs[1, :, span(i, 256)] = part[2 * rows:].astype(BF16)
 
     loop(feat // 256)(through)
-    back = (
-        start(qgs.at[0], qgr.at[0], X_OUT + 0, at(dx=1)),
-        start(qgs.at[1], qgr.at[1], X_OUT + 1, at(dx=2)),
-    )
+    operands.append(start(qq.at[1 - c, early], qqp.at[early], H_IN + 3, core))
+    sum_a(0)
     sum_b(1)
-    def head_part(which, out):
-        def one(i):
-            block = span(i, 256)
-            out(block, tn(xa[:, block], qq[which]))
-        loop(feat // 256)(one)
-
-    def give(block, value):
-        hcs[block, :] = value.astype(BF16)
-
-    head_part(1 - c, give)
-    hc = start(hcs, hcr, H_C, core)
-    sum_a(1)
-
-    def keep(block, value):
-        h2[block, :] = value
-
-    head_part(c, keep)
+    cross.wait_recv()
+    yown[...] = table_hard(0) + cr[...].astype(F32)
+    ys[0, lo] = yown[2, lo].astype(BF16)
+    ys[1, hi] = yown[2, hi].astype(BF16)
+    yrs = (
+        start(ys.at[0, lo], yr.at[0, lo], Y_RS + 0, yright),
+        start(ys.at[1, hi], yr.at[1, hi], Y_RS + 1, yleft),
+    )
     zown[7] = table_in(7)
     table_pair(0)
-    sum_b(2)
-    hc.wait_recv()
-
-    def join(i):
-        block = span(i, 128)
-        h2[block, :] = h2[block, :] + hcr[block, :].astype(F32)
-
-    loop(feat // 128)(join)
+    for one in operands:
+        one.wait_recv()
+
+    def head_part(i):
+        block = span(i, 256)
+        h2[block, :] = tn(xa[:, block], qq[c]) + tn(xap[:, block], qqp[...])
+
+    loop(feat // 256)(head_part)
 
     groups = feat // (8 * NY)
     view_a = h2.reshape(groups, NY, 8, fhalf)
@@ -453,32 +473,12 @@
         xh2, xl2 = cross_x(d)
         h1s[d + 2] = view_b[xh2, :, xl2, :, fq:fhalf].reshape(groups * 8, fq).astype(BF16)
         stage1.append(start(h1s.at[d + 2], h1r.at[d + 2], H_B1 + d - 1, at(dx=d)))
-    sum_a(2)
-
-    def table_hard(i):
-        return tn(g_hd[:, span(i, rows)], qp[pl.ds(0, 2 * rows), :])
-
-    def cross(i):
-        cs[i] = table_hard(NY + i).astype(BF16)
-
-    loop(NY)(cross)
-    crs = [start(cs.at[i], cr.at[i], C_RS + i, core) for i in range(NY)]
-    for one in crs:
-        one.wait_recv()
-
-    def own_hard(i):
-        yown[i] = table_hard(i) + cr[i].astype(F32)
-
-    loop(NY)(own_hard)
-    ys[0, lo] = yown[2, lo].astype(BF16)
-    ys[1, hi] = yown[2, hi].astype(BF16)
-    yrs = (
-        start(ys.at[0, lo], yr.at[0, lo], Y_RS + 0, yright),
-        start(ys.at[1, hi], yr.at[1, hi], Y_RS + 1, yleft),
-    )
+    sum_a(1)
+    sum_b(2)
 
     hm[0] = view_a[:, y, :, 0:fq].reshape(groups * 8, fq)
     hm[1] = view_b[xh, :, xl, :, fq:fhalf].reshape(groups * 8, fq)
+    sum_a(2)
     for one in stage1:
         one.wait_recv()
     for n in range(2):
@@ -504,8 +504,6 @@
         start(ys.at[2], yr.at[2], Y_RS + 2, yright),
         start(ys.at[3], yr.at[3], Y_RS + 3, yleft),
     )
-
-    arrive(rb[3])
     for one in stage2:
         one.wait_recv()
     small_a = part_a[xh, :, xl].reshape(NZ * 8, fq)
@@ -515,39 +513,41 @@
         small_b = small_b + h2r[d + 3].astype(F32)
     hzs[:, :, pl.ds(0, fq)] = small_a.reshape(NZ, 8, fq)
     hzs[:, :, pl.ds(fq, fq)] = small_b.reshape(NZ, 8, fq)
-    hz = [
-        start(hzs.at[lax.rem(z + d, NZ)], hzr.at[d - 1], H_Z + d - 1, at(dz=d))
-        for d in range(1, NZ)
-    ]
+    hz = [start(hzs.at[z], hzr.at[1, NZ - 1], H_Z + 2 * NZ - 2, core)]
+    for d in (4, 3, 5, 2, 6, 1, 7):
+        there = hzs.at[lax.rem(z + d, NZ)]
+        hz.append(start(there, hzr.at[0, d - 1], H_Z + d - 1, at(dz=d)))
+        hz.append(start(there, hzr.at[1, d - 1], H_Z + NZ - 2 + d, at(dz=d, dc=1)))
 
     arrive(back)
-    acc[...] = acc[...] + qgr[0].astype(F32) + qgr[1].astype(F32)
+    acc[...] = acc[...] + ar[0].astype(F32) + ar[1].astype(F32)
+
+    def question_in(i):
+        block = span(i, 256)
+        ar[0, :, block] = nn(acc[...].astype(BF16), head_ref[:, block]).astype(BF16)
 
     def question(i):
         block = span(i, 256)
-        gq_ref[:, block] = nt(acc[...].astype(BF16), head_ref[block, :]).astype(BF16)
-
+        gq_ref[:, block] = nt(ar[0], head_ref[block, :]).astype(BF16)
+
+    loop(feat // 256)(question_in)
     loop(feat // 256)(question)
 
-    for one in hz:
-        one.wait_recv()
-    last = hzs[z]
-    for d in range(NZ - 1):
-        last = last + hzr[d]
-    hc2s[...] = last
-    hc2 = start(hc2s, hc2r, H_C2, core)
-
+    arrive(rb[3])
     arrive(yrs2)
     zown[0] = (zown[0] + yown[0]) + (yr[2].astype(F32) + yr[3].astype(F32))
     arrive(ra[3])
     gt_ref[...] = (zown[0] + (zr[3].astype(F32) + zr[7].astype(F32))).astype(BF16)
 
-    hc2.wait_recv()
-    far = hc2r[...]
-    picked_own = jnp.where(c == 0, last[0:4], last[4:8])
-    picked = jnp.where(c == 0, far[0:4], far[4:8])
-    gh_ref[:, pl.ds(0, fhalf)] = jnp.where(c == 0, picked_own, picked)
-    gh_ref[:, pl.ds(fhalf, fhalf)] = jnp.where(c == 0, picked, picked_own)
+    for one in hz:
+        one.wait_recv()
+    near, far = hzs[z], hzr[1, NZ - 1]
+    for d in range(NZ - 1):
+        near, far = near + hzr[0, d], far + hzr[1, d]
+    near = jnp.where(c == 0, near[0:4], near[4:8])
+    far = jnp.where(c == 0, far[0:4], far[4:8])
+    gh_ref[:, pl.ds(0, fhalf)] = jnp.where(c == 0, near, far)
+    gh_ref[:, pl.ds(fhalf, fhalf)] = jnp.where(c == 0, far, near)
 
     for one in started:
         one.wait_send()
@@ -589,19 +589,16 @@
         ((4, rows, feat), BF16),
         ((rows, feat), F32),
         ((2, rows, feat), BF16),
-        ((2, rows, feat), BF16),
         ((feat, fhalf), F32),
-        ((feat, fhalf), BF16),
-        ((feat, fhalf), BF16),
+        ((6 * rows, feat), BF16),
+        ((6 * rows, fhalf), BF16),
         ((6, feat // NY, fq), BF16),
         ((6, feat // NY, fq), BF16),
         ((2, feat // NY, fq), F32),
         ((6, NZ * 8, fq), BF16),
         ((6, NZ * 8, fq), BF16),
         ((NZ, 8, fhalf), F32),
-        ((NZ - 1, 8, fhalf), F32),
-        ((8, fhalf), F32),
-        ((8, fhalf), F32),
+        ((2, NZ, 8, fhalf), F32),
     ]
     outs = (
         jax.ShapeDtypeStruct((rows, feat), BF16),

time: 81.2 us -> 80.3 us (0.989)
  no operation moved by 1% of the time
where the time goes in v3:
time: 80.3 us; the launch traced here: 80.2 us
  Pallas kernels  79.6 us (99%)
    pallas_call x1, Pallas kernels, body(): pl.pallas_call(kernel, out_shape=outs, in_specs=[vmem] * 6, out_specs=(vm...  77.7 us
    pallas_call x1, Pallas kernels, body(): pl.pallas_call(hand_over, out_shape=outs, in_specs=[vmem] * 3, out_specs=...  1.84 us

profile of v3, /device:TPU:1, one launch (start us, length us, event | category | flops | bytes accessed | tf_op | source)
XLA Modules:
  0.0 80.2 jit_solution(1719636060897522511)
XLA Ops:
  0.6 77.7 %shard_map.85 = (bf16[128,1024]{1,0:T(8,128)(2,1)}, bf16[128,1024]{1,0:T(8,128)(2,1)}, f32[4,1024]{1,0:T(4,128)}) custom-call(bf16[128,1024]{1,0:T(8,128)(2,1)} %bitcast.7, bf16[128,1024]{1,0:T(8,128)(2,1)} %bitcast.8, bf16[1024,1024]{1,0:T(8,128)(2,1)} %head_ref.1, f32[1,128]{1,0:T(1,128)} %weight_ref.1, s32[1,128]{1,0:T(1,128)} %positive_ref.1, ...), custom_call_target="tpu_custom_call" | custom-call | tf_op jit(solution)/shard_map/pallas_call | solution.py:608
  78.4 1.8 %shard_map.86 = (bf16[128,1024]{1,0:T(8,128)(2,1)}, bf16[128,1024]{1,0:T(8,128)(2,1)}, f32[4,1024]{1,0:T(4,128)}) custom-call(bf16[128,1024]{1,0:T(8,128)(2,1)} %get-tuple-element.9.refs_0_, bf16[128,1024]{1,0:T(8,128)(2,1)} %get-tuple-element.10.refs_1_, f32[4,1024]{1,0:T(4,128)} %get-tuple-element.11.refs_2_), custom_call_target="tpu_custom_call" | custom-call | tf_op jit(solution)/shard_map/pallas_call | solution.py:621

commit v4 on v3

--- a/solution.py
+++ b/solution.py
@@ -48,7 +48,7 @@
 def kernel(
     qe_ref, te_ref, head_ref, weight_ref, positive_ref, ids_ref, gq_ref, gt_ref, gh_ref,
     xa, qq, qp, tz, ty, meta, info, s_in, s_hd, g_in, g_hd, st_in, st_hd, stat, wide, alpha,
-    zs, zr, zown, cs, cr, yown, ys, yr, acc, ar,
+    zs, zr, zown, cs, cr, yown, ys, yr, acc, ar, br, qown,
     h2, xap, qqp, h1s, h1r, hm, h2s, h2r, hzs, hzr,
     send_sem, recv_sem,
 ):
@@ -192,6 +192,10 @@
         for k in range(4):
             count += jnp.where(named[:, 2 + k:3 + k] == hard_col, 1.0, 0.0)
         s_hd[block, :] = jnp.where(count > 0.0, jnp.log(jnp.maximum(count, 1.0)), NEG)
+
+    def score_hard(where, slot):
+        block = pl.ds(slot * rows, rows) if isinstance(slot, int) else span(slot, rows)
+        s_hd[where, block] = s_hd[where, block] + nt(qp[where, :], ty[slot])
 
     arrive(za[0])
     gather_a(1)
@@ -206,18 +210,14 @@
     cag.append(start(ty.at[3], ty.at[7], C_AG + 1, core))
     cag.append(start(ty.at[1], ty.at[5], C_AG + 2, core))
     loop(rows // 32)(lambda i: mask_hard(i + rows // 32))
+    for slot in (0, 3, 1):
+        score_hard(high, slot)
     arrive(za[1])
     gather_a(2)
     arrive(yag2)
     cag.append(start(ty.at[2], ty.at[6], C_AG + 3, core))
     arrive(zb[1])
     gather_b(2)
-
-    def score_hard(where):
-        def one(i):
-            block = span(i, rows)
-            s_hd[where, block] = s_hd[where, block] + nt(qp[where, :], ty[i])
-        loop(2 * NY)(one)
 
     def two_lanes(first, second):
         place = lax.broadcasted_iota(jnp.int32, (first.shape[0], 128), 1)
@@ -231,25 +231,23 @@
         s_hd[block, :] = prob
         st_hd[block, :] = two_lanes(top, jnp.sum(prob, axis=1, keepdims=True))
 
-    for one in cag:
-        one.wait_recv()
-    arrive(za[2])
-    gather_a(3)
-    score_hard(high)
-    loop(rows // 32)(lambda i: stats_hard(i + rows // 32))
-    for slot in (0, 7, 1, 6, 2):
-        score_in(slot, low, high)
     x1.wait_recv()
     x2.wait_recv()
     early, late = pl.ds(0, 3 * rows), pl.ds(3 * rows, 3 * rows)
     operands = [start(xa.at[early], xap.at[early], H_IN + 0, core)]
     project([0, 2])
     operands.append(start(qq.at[1 - c, late], qqp.at[late], H_IN + 1, core))
+    arrive(za[2])
+    gather_a(3)
     project_back([0, 2])
-    score_hard(low)
-    loop(rows // 32)(stats_hard)
+    for one in cag:
+        one.wait_recv()
+    loop(2 * NY)(functools.partial(score_hard, low))
+    for slot in (2, 4, 5, 6, 7):
+        score_hard(high, slot)
+    loop(2 * rows // 32)(stats_hard)
     for slot in (0, 7, 1, 6, 2):
-        score_in(slot, high, top_rows)
+        score_in(slot, pl.ds(0, 2 * rows), pl.ds(rows, 2 * rows))
     arrive(zb[2])
     for slot in (5, 3):
         score_in(slot, pl.ds(0, 2 * rows), pl.ds(rows, 2 * rows))
@@ -398,18 +396,18 @@
 
     loop(rows // 32)(grad_hard)
 
+    def table_hard(first):
+        many = tn(g_hd[:, pl.ds(first * rows, NY * rows)], qp[pl.ds(0, 2 * rows), :])
+        return many.reshape(NY, rows, feat)
+
+    cs[...] = table_hard(NY).astype(BF16)
+    cross = start(cs, cr, C_RS, core)
+
     table_pair(2)
     table_pair(5)
     zs[1, hi] = zown[3, hi].astype(BF16)
     zs[5, lo] = zown[5, lo].astype(BF16)
     reduce_b(1)
-
-    def table_hard(first):
-        many = tn(g_hd[:, pl.ds(first * rows, NY * rows)], qp[pl.ds(0, 2 * rows), :])
-        return many.reshape(NY, rows, feat)
-
-    cs[...] = table_hard(NY).astype(BF16)
-    cross = start(cs, cr, C_RS, core)
 
     def ahead(i):
         block = span(i, 256)
@@ -426,19 +424,8 @@
         xa[pl.ds(at0 + 2 * rows, rows), block] = (scale * a_in[rows:]).astype(BF16)
 
     loop(feat // 256)(ahead)
-    back = (
-        start(xa.at[pl.ds(3 * rows, rows)], ar.at[0], X_OUT + 0, at(dx=1)),
-        start(xa.at[pl.ds(5 * rows, rows)], ar.at[1], X_OUT + 1, at(dx=2)),
-    )
+    back1 = start(xa.at[pl.ds(3 * rows, rows)], ar.at[0], X_OUT + 0, at(dx=1))
     operands.append(start(xa.at[late], xap.at[late], H_IN + 2, core))
-    def through(i):
-        part = nn(xa[pl.ds(3 * rows, 3 * rows), :], head_ref[:, span(i, 256)])
-        qq[lax.div(i, 2), pl.ds(0, 3 * rows), span(lax.rem(i, 2), 256)] = part.astype(BF16)
-
-    loop(feat // 256)(through)
-    operands.append(start(qq.at[1 - c, early], qqp.at[early], H_IN + 3, core))
-    sum_a(0)
-    sum_b(1)
     cross.wait_recv()
     yown[...] = table_hard(0) + cr[...].astype(F32)
     ys[0, lo] = yown[2, lo].astype(BF16)
@@ -447,6 +434,15 @@
         start(ys.at[0, lo], yr.at[0, lo], Y_RS + 0, yright),
         start(ys.at[1, hi], yr.at[1, hi], Y_RS + 1, yleft),
     )
+
+    def through(i):
+        part = nn(xa[pl.ds(3 * rows, 3 * rows), :], head_ref[:, span(i, 256)])
+        qq[lax.div(i, 2), pl.ds(0, 3 * rows), span(lax.rem(i, 2), 256)] = part.astype(BF16)
+
+    loop(feat // 256)(through)
+    operands.append(start(qq.at[1 - c, early], qqp.at[early], H_IN + 3, core))
+    sum_a(0)
+    sum_b(1)
     zown[7] = table_in(7)
     table_pair(0)
     for one in operands:
@@ -479,6 +475,14 @@
     hm[0] = view_a[:, y, :, 0:fq].reshape(groups * 8, fq)
     hm[1] = view_b[xh, :, xl, :, fq:fhalf].reshape(groups * 8, fq)
     sum_a(2)
+    back1.wait_recv()
+    ar[0] = (acc[...] + ar[0].astype(F32)).astype(BF16)
+
+    def question_in(i):
+        block = span(i, 256)
+        qown[:, block] = nn(ar[0], head_ref[:, block])
+
+    loop(feat // 256)(question_in)
     for one in stage1:
         one.wait_recv()
     for n in range(2):
@@ -495,6 +499,7 @@
         there = lax.rem(y + d, NY)
         h2s[d + 2] = part_b[:, there].reshape(NZ * 8, fq).astype(BF16)
         stage2.append(start(h2s.at[d + 2], h2r.at[d + 2], H_B2 + d - 1, at(dy=d)))
+    back2 = start(qq.at[:, pl.ds(2 * rows, rows)], br, X_OUT + 1, at(dx=2))
     arrive(yrs)
     ys[2, lo] = (yown[1, lo] + yr[0, lo].astype(F32)).astype(BF16)
     ys[2, hi] = yown[1, hi].astype(BF16)
@@ -519,18 +524,15 @@
         hz.append(start(there, hzr.at[0, d - 1], H_Z + d - 1, at(dz=d)))
         hz.append(start(there, hzr.at[1, d - 1], H_Z + NZ - 2 + d, at(dz=d, dc=1)))
 
-    arrive(back)
-    acc[...] = acc[...] + ar[0].astype(F32) + ar[1].astype(F32)
-
-    def question_in(i):
-        block = span(i, 256)
-        ar[0, :, block] = nn(acc[...].astype(BF16), head_ref[:, block]).astype(BF16)
+    back2.wait_recv()
+    for h in range(2):
+        part = pl.ds(h * fhalf, fhalf)
+        ar[1, :, part] = (qown[:, part] + br[h].astype(F32)).astype(BF16)
 
     def question(i):
         block = span(i, 256)
-        gq_ref[:, block] = nt(ar[0], head_ref[block, :]).astype(BF16)
-
-    loop(feat // 256)(question_in)
+        gq_ref[:, block] = nt(ar[1], head_ref[block, :]).astype(BF16)
+
     loop(feat // 256)(question)
 
     arrive(rb[3])
@@ -589,6 +591,8 @@
         ((4, rows, feat), BF16),
         ((rows, feat), F32),
         ((2, rows, feat), BF16),
+        ((2, rows, fhalf), BF16),
+        ((rows, feat), F32),
         ((feat, fhalf), F32),
         ((6 * rows, feat), BF16),
         ((6 * rows, fhalf), BF16),

time: 80.3 us -> 76.5 us (0.953)
  Pallas kernels: 79.6 us -> 75.7 us
    pallas_call x1, Pallas kernels: 77.7 us -> 73.9 us  [body(): pl.pallas_call(kernel, out_shape=outs, in_specs=[vmem] * 6, out_specs=(vm...]
where the time goes in v4:
time: 76.5 us; the launch traced here: 76.4 us
  Pallas kernels  75.7 us (99%)
    pallas_call x1, Pallas kernels, body(): pl.pallas_call(kernel, out_shape=outs, in_specs=[vmem] * 6, out_specs=(vm...  73.9 us
    pallas_call x1, Pallas kernels, body(): pl.pallas_call(hand_over, out_shape=outs, in_specs=[vmem] * 3, out_specs=...  1.84 us

profile of v4, /device:TPU:1, one launch (start us, length us, event | category | flops | bytes accessed | tf_op | source)
XLA Modules:
  0.0 76.4 jit_solution(10706011228323607039)
XLA Ops:
  0.6 73.9 %shard_map.85 = (bf16[128,1024]{1,0:T(8,128)(2,1)}, bf16[128,1024]{1,0:T(8,128)(2,1)}, f32[4,1024]{1,0:T(4,128)}) custom-call(bf16[128,1024]{1,0:T(8,128)(2,1)} %bitcast.7, bf16[128,1024]{1,0:T(8,128)(2,1)} %bitcast.8, bf16[1024,1024]{1,0:T(8,128)(2,1)} %head_ref.1, f32[1,128]{1,0:T(1,128)} %weight_ref.1, s32[1,128]{1,0:T(1,128)} %positive_ref.1, ...), custom_call_target="tpu_custom_call" | custom-call | tf_op jit(solution)/shard_map/pallas_call | solution.py:612
  74.5 1.8 %shard_map.86 = (bf16[128,1024]{1,0:T(8,128)(2,1)}, bf16[128,1024]{1,0:T(8,128)(2,1)}, f32[4,1024]{1,0:T(4,128)}) custom-call(bf16[128,1024]{1,0:T(8,128)(2,1)} %get-tuple-element.9.refs_0_, bf16[128,1024]{1,0:T(8,128)(2,1)} %get-tuple-element.10.refs_1_, f32[4,1024]{1,0:T(4,128)} %get-tuple-element.11.refs_2_), custom_call_target="tpu_custom_call" | custom-call | tf_op jit(solution)/shard_map/pallas_call | solution.py:625

commit v5 on v4

--- a/solution.py
+++ b/solution.py
@@ -300,7 +300,7 @@
     stat[0, 2:3, :], stat[0, 3:4, :] = theirs
     stat[0, 4:6, :] = wide[10:12, :]
     stat[0, 6:8, :] = jnp.zeros((2, rows), F32)
-    shared = [start(stat.at[0], stat.at[d], STAT + d - 1, at(dx=d)) for d in (1, 2, 3)]
+    shared = [start(stat.at[0], stat.at[d], STAT + d - 1, at(dx=d)) for d in (2, 1, 3)]
     for one in shared:
         one.wait_recv()
 
@@ -462,7 +462,7 @@
         return (1 - xh if d & 2 else xh), (1 - xl if d & 1 else xl)
 
     stage1 = []
-    for d in (1, 2, 3):
+    for d in (2, 1, 3):
         there = lax.rem(y + d, NY)
         h1s[d - 1] = view_a[:, there, :, 0:fq].reshape(groups * 8, fq).astype(BF16)
         stage1.append(start(h1s.at[d - 1], h1r.at[d - 1], H_A1 + d - 1, at(dy=d)))
@@ -492,7 +492,7 @@
     part_a = hm.at[0].reshape(2, NZ, 2, 8, fq)
     part_b = hm.at[1].reshape(NZ, NY, 8, fq)
     stage2 = []
-    for d in (1, 2, 3):
+    for d in (2, 1, 3):
         xh2, xl2 = cross_x(d)
         h2s[d - 1] = part_a[xh2, :, xl2].reshape(NZ * 8, fq).astype(BF16)
         stage2.append(start(h2s.at[d - 1], h2r.at[d - 1], H_A2 + d - 1, at(dx=d)))

time: 76.5 us -> 76.7 us (level)
  no operation moved by 1% of the time
where the time goes in v5:
time: 76.7 us; the launch traced here: 76.5 us
  Pallas kernels  75.9 us (99%)
    pallas_call x1, Pallas kernels, body(): pl.pallas_call(kernel, out_shape=outs, in_specs=[vmem] * 6, out_specs=(vm...  74.1 us
    pallas_call x1, Pallas kernels, body(): pl.pallas_call(hand_over, out_shape=outs, in_specs=[vmem] * 3, out_specs=...  1.84 us

profile of v5, /device:TPU:1, one launch (start us, length us, event | category | flops | bytes accessed | tf_op | source)
XLA Modules:
  0.0 76.5 jit_solution(2215040784567051347)
XLA Ops:
  0.6 74.1 %shard_map.85 = (bf16[128,1024]{1,0:T(8,128)(2,1)}, bf16[128,1024]{1,0:T(8,128)(2,1)}, f32[4,1024]{1,0:T(4,128)}) custom-call(bf16[128,1024]{1,0:T(8,128)(2,1)} %bitcast.7, bf16[128,1024]{1,0:T(8,128)(2,1)} %bitcast.8, bf16[1024,1024]{1,0:T(8,128)(2,1)} %head_ref.1, f32[1,128]{1,0:T(1,128)} %weight_ref.1, s32[1,128]{1,0:T(1,128)} %positive_ref.1, ...), custom_call_target="tpu_custom_call" | custom-call | tf_op jit(solution)/shard_map/pallas_call | solution.py:612
  74.7 1.8 %shard_map.86 = (bf16[128,1024]{1,0:T(8,128)(2,1)}, bf16[128,1024]{1,0:T(8,128)(2,1)}, f32[4,1024]{1,0:T(4,128)}) custom-call(bf16[128,1024]{1,0:T(8,128)(2,1)} %get-tuple-element.9.refs_0_, bf16[128,1024]{1,0:T(8,128)(2,1)} %get-tuple-element.10.refs_1_, f32[4,1024]{1,0:T(4,128)} %get-tuple-element.11.refs_2_), custom_call_target="tpu_custom_call" | custom-call | tf_op jit(solution)/shard_map/pallas_call | solution.py:625
